TPU v7x, 256 devices: a whole 4x4x8 slice. The times are simulated.
256 devices in a mesh: resp: 32 (over z, y_hi, core), head: 8 (over y_lo, x).
Axes of the slice: x: 4, y: 4 (y_hi: 2, y_lo: 2; y = y_hi * 2 + y_lo), z: 8, core: 2. Of those that a mesh axis runs over, the one named last changes fastest.
Arguments:
- queries: bfloat16 [8192, 4096], P('resp', 'head'), may hold values from -512 to 512
- resp_keys: bfloat16 [8192, 1024], P('resp', 'head'), may hold values from -6 to 6
- resp_values: bfloat16 [8192, 1024], P('resp', 'head'), may hold values from -6 to 6
- prompt_keys: bfloat16 [16384, 1024], P('resp', 'head'), may hold values from -6 to 6
- prompt_values: bfloat16 [16384, 1024], P('resp', 'head'), may hold values from -6 to 6
- lengths: int32 [128], P('resp'), may hold values from 1 to 64, as said below
- out_weight: bfloat16 [4096, 8192], P('head'), may hold values from -0.5 to 0.5
Outputs:
- mixed: bfloat16 [8192, 8192], P('resp', 'head')
Inputs may be any that keep to these rules, and one draw needn't show every extreme that they name: `lengths`: every response has between 1 and 64 live tokens, and some response has all 64.
All inputs are finite; a program needn't handle non-finite values.
Results may differ from a plain program's by a relative error of at most 0.02.
Values may be sent and summed in bfloat16 or wider, within the bound.
No kernel may reach another device: no remote copies, remote signals or barrier semaphores. Data moves between devices by JAX's collectives and lax.ppermute only.
A program may use at most 64 MiB of HBM per device.

v0:
```python
import functools
import math

import jax
import jax.numpy as jnp
from jax import lax
from jax.experimental import pallas as pl
from jax.experimental.pallas import tpu as pltpu
from jax.sharding import Mesh, PartitionSpec as P

NEG = -1e30
NT = (((1,), (1,)), ((), ()))


def ring(size, step):
    return [(i, (i + step) % size) for i in range(size)]


def opposite(size, step):
    pairs = []
    for place in range(size):
        pairs.append((2 * place, 2 * ((place + step) % size)))
        pairs.append((2 * place + 1, 2 * ((place - step) % size) + 1))
    return pairs


def opposite_x(size, step):
    forward = [(i, (i + step) % size) for i in range(size)]
    backward = [(size + i, size + (i - step) % size) for i in range(size)]
    return forward + backward


def lanes(x, width):
    return x if width == x.shape[1] else jnp.concatenate([x] * (width // x.shape[1]), 1)


def with_ones(values):
    return jnp.concatenate([values, jnp.ones((values.shape[0], 128), jnp.bfloat16)], 1)


def fold(tiles, scale, query, blocks, read, write, extra=None):
    keys = [block[:, :128] for block in blocks]
    values = [with_ones(block[:, 128:]) for block in blocks]

    def score(tile):
        return [
            lax.dot_general(query(tile), key, NT, preferred_element_type=jnp.float32)
            for key in keys
        ]

    def finish(item):
        tile, pairs, shrink, top, old = item
        total = None
        for weight, value in pairs:
            term = jnp.dot(weight, value, preferred_element_type=jnp.float32)
            total = term if total is None else total + term
        accum, count = total[:, :128], total[:, 128:]
        if old is not None:
            accum = accum + old[0] * shrink
            count = count + old[2] * shrink
        write(tile, accum, top, count)

    upcoming = score(tiles[0])
    waiting = None
    for place, tile in enumerate(tiles):
        scores, sides = upcoming, values
        if place + 1 < len(tiles):
            upcoming = score(tiles[place + 1])
        if waiting is not None:
            finish(waiting)
        own = extra(tile) if extra is not None else None
        if own is not None:
            scores, sides = scores + [own[0]], sides + [own[1]]
        peak = None
        for part in scores:
            for at in range(0, part.shape[1], 128):
                column = part[:, at : at + 128]
                peak = column if peak is None else jnp.maximum(peak, column)
        top = jnp.broadcast_to(jnp.max(peak, 1, keepdims=True), peak.shape) * scale
        old = read(tile)
        shrink = None
        if old is not None:
            top = jnp.maximum(top, old[1])
            shrink = jnp.exp2(old[1] - top)
        weights = [
            jnp.exp2(part * scale - lanes(top, part.shape[1])).astype(jnp.bfloat16)
            for part in scores
        ]
        waiting = (tile, list(zip(weights, sides)), shrink, top, old)
    finish(waiting)


def live_of(lengths, index, resp_len, count):
    live = jnp.zeros(index.shape, jnp.int32)
    for response in range(count):
        live = jnp.where(index // resp_len == response, lengths[response], live)
    return live


def attend_kernel(scale, group, resp_len, sets, rows_of, first, with_self, *refs):
    refs = list(refs)
    lengths, own_keys, own_values = [refs.pop(0) for _ in range(3)] if with_self else [None] * 3
    queries = [refs.pop(0) for _ in range(sets)]
    blocks = [refs.pop(0)[:rows, :] for rows in rows_of]
    old = None if first else [[refs.pop(0) for _ in range(3)] for _ in range(sets)]
    new = [[refs.pop(0) for _ in range(3)] for _ in range(sets)]
    slots = queries[0].shape[0]
    turns = 2

    def at(tile):
        return pl.ds(pl.multiple_of(tile[1] * slots, slots), slots)

    def query(tile):
        return queries[tile[0]][:, pl.ds(pl.multiple_of(tile[1] * 128, 128), 128)]

    def read(tile):
        return None if first else [ref[at(tile), :] for ref in old[tile[0]]]

    def write(tile, *state):
        for ref, value in zip(new[tile[0]], state):
            ref[at(tile), :] = value

    extra = None
    if with_self:
        shape = (slots, slots)
        slot = lax.broadcasted_iota(jnp.int32, shape, 0)
        other = lax.broadcasted_iota(jnp.int32, shape, 1)
        keep = (slot // resp_len == other // resp_len) & (other <= slot)
        keep = keep & (other % resp_len < live_of(lengths, other, resp_len, slots // resp_len))
        own_sums = with_ones(own_values[...])

        def extra(tile):
            scores = lax.dot_general(
                query(tile), own_keys[...], NT, preferred_element_type=jnp.float32
            )
            return jnp.where(keep, scores, NEG), own_sums

    def turn(index, _):
        heads = [index * (group // turns) + head for head in range(group // turns)]
        tiles = [(place, head) for place in range(sets) for head in heads]
        fold(tiles, scale, query, blocks, read, write, extra)
        return 0

    if turns == 1:
        turn(0, 0)
    else:
        lax.fori_loop(0, turns, turn, 0)


VMEM = pl.BlockSpec(memory_space=pltpu.VMEM)
SMEM = pl.BlockSpec(memory_space=pltpu.SMEM)


def params(mebibytes=32):
    return pltpu.CompilerParams(vmem_limit_bytes=mebibytes * 2**20)


def attend(scale, group, resp_len, queries, blocks, states=None, own=None, work=16):
    sets, slots = len(queries), queries[0].shape[0]
    rows = slots * group
    first = states is None
    operands = list(own or []) + list(queries) + [block for block, _ in blocks]
    keys = sum(count for _, count in blocks)
    state = jax.ShapeDtypeStruct((rows, 128), jnp.float32)
    aliases = {}
    if not first:
        aliases = {len(operands) + i: i for i in range(3 * sets)}
        operands += [array for one in states for array in one]
    specs = [VMEM] * len(operands)
    if own:
        specs[0] = SMEM
    out = pl.pallas_call(
        functools.partial(
            attend_kernel, scale, group, resp_len, sets, [count for _, count in blocks], first, bool(own)
        ),
        in_specs=specs,
        out_specs=[VMEM] * (3 * sets),
        out_shape=[state] * (3 * sets),
        input_output_aliases=aliases,
        compiler_params=params(),
        cost_estimate=pl.CostEstimate(
            flops=work * sets * rows * keys * 128, bytes_accessed=2**16, transcendentals=0
        ),
        name="attend",
    )(*operands)
    return [out[3 * i : 3 * i + 3] for i in range(sets)]


def ship_kernel(group, acc, top, total, out, stats):
    slots = out.shape[0]
    lane = lax.broadcasted_iota(jnp.int32, (slots, 128), 1) // 16
    packed = jnp.zeros((slots, 128), jnp.float32)
    for head in range(group):
        at = pl.ds(head * slots, slots)
        out[:, head * 128 : (head + 1) * 128] = (acc[at, :] / total[at, :]).astype(jnp.bfloat16)
        packed = jnp.where(lane == head, top[at, :], packed)
        packed = jnp.where(lane == group + head, total[at, :], packed)
    stats[...] = packed


def ship(group, state):
    slots = state[0].shape[0] // group
    return pl.pallas_call(
        functools.partial(ship_kernel, group),
        in_specs=[VMEM] * 3,
        out_specs=[VMEM] * 2,
        out_shape=[
            jax.ShapeDtypeStruct((slots, group * 128), jnp.bfloat16),
            jax.ShapeDtypeStruct((slots, 128), jnp.float32),
        ],
        compiler_params=params(),
        name="ship",
    )(*state)


def merge_kernel(group, resp_len, lengths, acc, top, total, other, stats, *outs):
    slots = other.shape[0]
    part = slots // len(outs)
    slot = lax.broadcasted_iota(jnp.int32, (slots, 128), 0)
    alive = slot % resp_len < live_of(lengths, slot, resp_len, slots // resp_len)
    for head in range(group):
        at = pl.ds(head * slots, slots)
        columns = slice(head * 128, (head + 1) * 128)
        shape = (slots, 128)
        other_top = jnp.broadcast_to(stats[:, head * 16 : head * 16 + 1], shape)
        place = (group + head) * 16
        other_total = jnp.broadcast_to(stats[:, place : place + 1], shape)
        peak = jnp.maximum(top[at, :], other_top)
        own = jnp.exp2(top[at, :] - peak)
        share = jnp.exp2(other_top - peak) * other_total
        accum = acc[at, :] * own + other[:, columns].astype(jnp.float32) * share
        result = jnp.where(alive, accum / (total[at, :] * own + share), 0.0)
        for index, out in enumerate(outs):
            out[:, columns] = result[index * part : (index + 1) * part].astype(jnp.bfloat16)


def merge(group, resp_len, lengths, state, other, stats):
    return pl.pallas_call(
        functools.partial(merge_kernel, group, resp_len),
        in_specs=[SMEM] + [VMEM] * 5,
        out_specs=[VMEM] * 2,
        out_shape=[jax.ShapeDtypeStruct((other.shape[0] // 2, other.shape[1]), jnp.bfloat16)] * 2,
        compiler_params=params(),
        name="merge",
    )(lengths, *state, other, stats)


def cut_kernel(places, weight, near, far, own, sems):
    rows, width = weight.shape[0], near.shape[1]
    depth = rows // 2
    copies = []
    for block in range(2):
        for out, count, start, column in (
            (near, rows, 0, places[block]),
            (far, depth, places[6], places[2 + block]),
            (own, rows, 0, places[4 + block]),
        ):
            source = weight.at[
                pl.ds(pl.multiple_of(start, depth), count),
                pl.ds(pl.multiple_of(column, width), width),
            ]
            target = out.at[pl.ds(block * count, count), :]
            copies.append(pltpu.make_async_copy(source, target, sems.at[len(copies)]))
    for copy in copies:
        copy.start()
    for copy in copies:
        copy.wait()


def cut(places, weight, width):
    rows = weight.shape[0]
    shapes = [jax.ShapeDtypeStruct((count, width), weight.dtype) for count in (2 * rows, rows, 2 * rows)]
    return pl.pallas_call(
        cut_kernel,
        in_specs=[SMEM, pl.BlockSpec(memory_space=pltpu.HBM)],
        out_specs=[VMEM] * 3,
        out_shape=shapes,
        scratch_shapes=[pltpu.SemaphoreType.DMA((6,))],
        compiler_params=params(46),
        name="cut",
    )(places, weight)


def project_kernel(block, core, own, first, second, far, w_own, w_first, w_second, w_mine, w_other, out):
    rows = w_own.shape[0] // 2
    depth = rows // 2

    def product(left, weight):
        return jnp.dot(left, weight, preferred_element_type=jnp.float32)

    total = None
    for left, weight in ((own, w_own), (first, w_first), (second, w_second)):
        term = product(left[...], weight[block * rows : (block + 1) * rows, :])
        total = term if total is None else total + term
    for at, weight in ((core[0], w_mine), (1 - core[0], w_other)):
        left = far[:, pl.ds(pl.multiple_of(at * depth, depth), depth)]
        total = total + product(left, weight[block * depth : (block + 1) * depth, :])
    out[...] = total.astype(jnp.bfloat16)


def project(block, core, inputs, weights):
    return pl.pallas_call(
        functools.partial(project_kernel, block),
        in_specs=[SMEM] + [VMEM] * (len(inputs) + len(weights)),
        out_specs=VMEM,
        out_shape=jax.ShapeDtypeStruct((inputs[0].shape[0], weights[0].shape[1]), jnp.bfloat16),
        compiler_params=params(),
        name="project",
    )(jnp.reshape(core, (1,)), *inputs, *weights)


def per_device(queries, resp_keys, resp_values, prompt_keys, prompt_values, lengths, out_weight):
    head_size = prompt_keys.shape[1]
    slots = queries.shape[0]
    group = queries.shape[1] // head_size
    resp_len = slots // lengths.shape[0]
    scale = head_size ** (-0.5) * math.log2(math.e)
    z_size = lax.axis_size("z")
    x_size = lax.axis_size("x")
    core = lax.axis_index("core")
    x_at = lax.axis_index("x")
    yl_at = lax.axis_index("yl")

    swap_core = lambda v: lax.ppermute(v, "core", ring(2, 1))
    swap_yh = lambda v: lax.ppermute(v, "yh", ring(2, 1))
    swap_yl = lambda v: lax.ppermute(v, "yl", ring(2, 1))
    z_hop = lambda v: lax.ppermute(v, ("z", "core"), opposite(z_size, 1))
    x_near = lambda v: lax.ppermute(v, ("core", "x"), opposite_x(x_size, 1))
    x_back = lambda v: lax.ppermute(v, ("core", "x"), opposite_x(x_size, -1))
    x_far = lambda v: lax.ppermute(v, "x", ring(x_size, 2))

    after = lax.optimization_barrier

    half = prompt_keys.shape[0]
    full = 2 * half
    keys_core, values_core = swap_core(prompt_keys), swap_core(prompt_values)
    q_core = swap_core(queries)
    kv = after(jnp.concatenate([prompt_keys, prompt_values], 1))
    kv_y = swap_yh(kv)
    pair = jnp.concatenate([kv, jnp.concatenate([keys_core, values_core], 1)], 0)
    pair = after(pair)
    a_1 = z_hop(pair)

    share = out_weight.shape[1] // (x_size * 2)
    x_next = (x_at + jnp.where(core == 0, 1, x_size - 1)) % x_size
    x_after = (x_at + 2) % x_size
    places = [
        (yl * x_size + x_to) * share for x_to in (x_next, x_after, x_at) for yl in (yl_at, 1 - yl_at)
    ]
    places = jnp.stack(places + [core * (out_weight.shape[0] // 2)]).astype(jnp.int32)

    query_sets = [queries, q_core]
    run = functools.partial(attend, scale, group, resp_len)

    def step(states, *blocks):
        return run(query_sets, blocks, states)

    def ordered(states, *arrays):
        flat, arrays = after((states, arrays))
        return flat, *arrays

    theirs = run([q_core], [(pair, half)], work=8)
    theirs, pair = ordered(theirs, pair)
    states = run([queries], [(pair, half)], None, (lengths, resp_keys, resp_values), work=8) + theirs
    states, places = ordered(states, places)
    w_near, w_far, w_own = cut(places, out_weight, share)
    w_far = x_near(w_far)
    states, a_1 = ordered(states, a_1)
    a_2 = z_hop(a_1)
    b_1 = swap_yh(a_1)
    states = run(query_sets, [(a_1, full)], states, work=32)
    states, kv_y, w_near = ordered(states, kv_y, w_near)
    w_near = x_near(w_near)
    states = run(query_sets, [(kv_y, half)], states, work=32)
    states, a_2 = ordered(states, a_2)
    a_3 = z_hop(a_2)
    b_2 = swap_yh(a_2)
    states = step(states, (a_2, full))
    states, b_1 = ordered(states, b_1)
    states = step(states, (b_1, full))
    states, a_3, w_far = ordered(states, a_3, w_far)
    w_far = x_near(w_far)
    a_4 = z_hop(a_3[:half])
    states = step(states, (a_3, full))
    states, b_2, a_4 = ordered(states, b_2, a_4)
    b_3 = z_hop(b_2)
    b_4 = swap_yh(a_4)
    states = run(query_sets, [(b_2, full), (a_4, half)], states, work=6)
    states, b_3, b_4, w_near = ordered(states, b_3, b_4, w_near)
    w_back = swap_core(w_near)
    last = [(b_3, full), (b_4, half)]
    theirs = run([q_core], last, [states[1]])[0]
    sent, stats = ship(group, theirs)
    own, sent, stats = ordered(states[0], sent, stats)
    got, got_stats = swap_core(sent), swap_core(stats)
    own = run([queries], last, [own])[0]
    attended = merge(group, resp_len, lengths, own, got, got_stats)

    attended, w_far = after((attended, w_far))
    w_other = swap_core(w_far)
    gathered = [[rows, x_near(rows), x_back(rows), x_far(rows)] for rows in attended]
    weights = [w_own, w_near, w_back, w_far, w_other]
    away = [project(1, core, rows, weights) for rows in gathered]
    arrived = [swap_yl(rows) for rows in away]
    kept = [project(0, core, rows, weights) for rows in gathered]
    kept, arrived = jnp.concatenate(kept, 0), jnp.concatenate(arrived, 0)
    return (kept.astype(jnp.float32) + arrived.astype(jnp.float32)).astype(jnp.bfloat16)


def solution(mesh):
    fine = Mesh(mesh.devices.reshape(8, 2, 2, 2, 4), ("z", "yh", "core", "yl", "x"))
    resp, head = ("z", "yh", "core"), ("yl", "x")
    return jax.shard_map(
        per_device,
        mesh=fine,
        in_specs=(P(resp, head),) * 5 + (P(resp), P(head, None)),
        out_specs=P(resp, head),
        check_vma=False,
    )
```

profile of v0, /device:TPU:8, one launch (start us, length us, event | category | flops | bytes accessed | tf_op | source)
XLA Modules:
  0.0 94.2 jit_solution(529442002023771325)
XLA Ops:
  1.9 2.0 %collective-permute-start.3 = (bf16[1024,256]{1,0:T(8,128)(2,1)S(1)}, bf16[1024,256]{1,0:T(8,128)(2,1)S(1)}, u32[]{:S(2)}, u32[]{:S(2)}) collective-permute-start(bf16[1024,256]{1,0:T(8,128)(2,1)S(1)} %maximum_maximum_fusion.refs_1_.refs_4_), channel_id=1, source_target_pairs={{0,32},{8,232},{32,64},{40,8},{64,96},{72,40},{96,128},{104,72},{1... | collective-permute-start | bytes 1572872 | tf_op jit(solution)/shard_map/ppermute | solution.py:327
  3.9 4.0 %collective-permute-start = (bf16[256,512]{1,0:T(8,128)(2,1)}, bf16[256,512]{1,0:T(8,128)(2,1)S(1)}, u32[]{:S(2)}, u32[]{:S(2)}) collective-permute-start(bf16[256,512]{1,0:T(8,128)(2,1)} %refs_0_.15), channel_id=1, source_target_pairs={{0,8},{8,0},{1,9},{9,1},{2,10},{10,2},{3,11},{11,3},{4,12},{12,4},... | collective-permute-start | bytes 786440 | tf_op jit(solution)/shard_map/ppermute | solution.py:324
  7.9 2.3 %collective-permute-start.4 = (bf16[512,256]{1,0:T(8,128)(2,1)S(1)}, bf16[512,256]{1,0:T(8,128)(2,1)S(1)}, u32[]{:S(2)}, u32[]{:S(2)}) collective-permute-start(bf16[512,256]{1,0:T(8,128)(2,1)S(1)} %pad_maximum_fusion), channel_id=1, source_target_pairs={{0,16},{16,0},{1,17},{17,1},{2,18},{18,2},{3,19},{19,3},{4,20},{20... | collective-permute-start | bytes 786440 | tf_op jit(solution)/shard_map/ppermute | solution.py:325
  10.3 1.4 %attend.10 = (f32[1024,128]{1,0:T(8,128)S(1)}, f32[1024,128]{1,0:T(8,128)S(1)}, f32[1024,128]{1,0:T(8,128)S(1)}) custom-call(bf16[256,512]{1,0:T(8,128)(2,1)S(1)} %collective-permute-done.refs_0_.refs_1_, bf16[1024,256]{1,0:T(8,128)(2,1)S(1)} %maximum_maximum_fusion.refs_1_.refs_4_), custom_call_target="tpu_custom_call" | custom-call | flops 536870912 | bytes 65536 | tf_op jit(solution)/shard_map/attend/pallas_call | solution.py:172
  11.7 2.1 %attend.11 = (f32[1024,128]{1,0:T(8,128)S(1)}, f32[1024,128]{1,0:T(8,128)S(1)}, f32[1024,128]{1,0:T(8,128)S(1)}) custom-call(s32[4]{0:T(128)S(1)} %copy-done, bf16[256,128]{1,0:T(8,128)(2,1)S(1)} %copy-done.2, bf16[256,128]{1,0:T(8,128)(2,1)S(1)} %copy-done.3, bf16[256,512]{1,0:T(8,128)(2,1)S(1)} %copy-done.1, ...), custom_call_target="tpu_custom_call" | custom-call | flops 536870912 | bytes 65536 | tf_op jit(solution)/shard_map/attend/pallas_call | solution.py:172
  13.8 3.1 %cut.1 = (bf16[1024,1024]{1,0:T(8,128)(2,1)S(1)}, bf16[512,1024]{1,0:T(8,128)(2,1)S(1)}, bf16[1024,1024]{1,0:T(8,128)(2,1)S(1)}) custom-call(s32[7]{0:T(128)S(1)} %stack.31.places, bf16[512,8192]{1,0:T(8,128)(2,1)} %weight.1), custom_call_target="tpu_custom_call" | custom-call | tf_op jit(solution)/shard_map/cut/pallas_call | solution.py:273
  16.9 1.6 %collective-permute-start.8 = (bf16[512,1024]{1,0:T(8,128)(2,1)S(1)}, bf16[512,1024]{1,0:T(8,128)(2,1)S(1)}, u32[]{:S(2)}, u32[]{:S(2)}) collective-permute-start(bf16[512,1024]{1,0:T(8,128)(2,1)S(1)} %get-tuple-element.203), channel_id=1, source_target_pairs={{0,1},{1,2},{2,3},{3,0},{8,11},{9,8},{10,9},{11,10},{4,5},{5,6},{6... | collective-permute-start | bytes 3145736 | tf_op jit(solution)/shard_map/ppermute | solution.py:328
  18.5 1.3 %collective-permute-start.6 = (bf16[1024,256]{1,0:T(8,128)(2,1)S(1)}, bf16[1024,256]{1,0:T(8,128)(2,1)S(1)}, u32[]{:S(2)}, u32[]{:S(2)}) collective-permute-start(bf16[1024,256]{1,0:T(8,128)(2,1)S(1)} %collective-permute-done.3.refs_2_), channel_id=1, source_target_pairs={{0,16},{16,0},{1,17},{17,1},{2,18},{18,2},{3,19},{19,3},{4,20},{20... | collective-permute-start | bytes 1572872 | tf_op jit(solution)/shard_map/ppermute | solution.py:325
  19.8 3.4 %attend.12 = (f32[1024,128]{1,0:T(8,128)S(1)}, f32[1024,128]{1,0:T(8,128)S(1)}, f32[1024,128]{1,0:T(8,128)S(1)}, f32[1024,128]{1,0:T(8,128)S(1)}, f32[1024,128]{1,0:T(8,128)S(1)}, /*index=5*/f32[1024,128]{1,0:T(8,128)S(1)}) custom-call(bf16[256,512]{1,0:T(8,128)(2,1)S(1)} %copy-done.1, ...), custom_call_target="tpu_custom_call", output_to_operand_aliasing={{0}: (3, {}), {1}: (4, {}), {2}: (5, {}), {3}: (6, {}), {4}... | custom-call | flops 8589934592 | bytes 65536 | tf_op jit(solution)/shard_map/attend/pallas_call | solution.py:172
  23.2 1.6 %collective-permute-start.13 = (bf16[1024,1024]{1,0:T(8,128)(2,1)S(1)}, bf16[1024,1024]{1,0:T(8,128)(2,1)S(1)}, u32[]{:S(2)}, u32[]{:S(2)}) collective-permute-start(bf16[1024,1024]{1,0:T(8,128)(2,1)S(1)} %get-tuple-element.231), channel_id=1, source_target_pairs={{0,1},{1,2},{2,3},{3,0},{8,11},{9,8},{10,9},{11,10},{4,5},{5,6},{6... | collective-permute-start | bytes 6291464 | tf_op jit(solution)/shard_map/ppermute | solution.py:328
  24.8 2.0 %attend.13 = (f32[1024,128]{1,0:T(8,128)S(1)}, f32[1024,128]{1,0:T(8,128)S(1)}, f32[1024,128]{1,0:T(8,128)S(1)}, f32[1024,128]{1,0:T(8,128)S(1)}, f32[1024,128]{1,0:T(8,128)S(1)}, /*index=5*/f32[1024,128]{1,0:T(8,128)S(1)}) custom-call(bf16[256,512]{1,0:T(8,128)(2,1)S(1)} %copy-done.1, ...), custom_call_target="tpu_custom_call", output_to_operand_aliasing={{0}: (3, {}), {1}: (4, {}), {2}: (5, {}), {3}: (6, {}), {4}... | custom-call | flops 4294967296 | bytes 65536 | tf_op jit(solution)/shard_map/attend/pallas_call | solution.py:172
  26.8 2.0 %collective-permute-done.5.refs_2_ = bf16[1024,256]{1,0:T(8,128)(2,1)S(1)} collective-permute-done((bf16[1024,256]{1,0:T(8,128)(2,1)S(1)}, bf16[1024,256]{1,0:T(8,128)(2,1)S(1)}, u32[]{:S(2)}, u32[]{:S(2)}) %collective-permute-start.5) | collective-permute-done | bytes 524320 | tf_op jit(solution)/shard_map/ppermute | solution.py:327
  30.2 3.4 %attend.14 = (f32[1024,128]{1,0:T(8,128)S(1)}, f32[1024,128]{1,0:T(8,128)S(1)}, f32[1024,128]{1,0:T(8,128)S(1)}, f32[1024,128]{1,0:T(8,128)S(1)}, f32[1024,128]{1,0:T(8,128)S(1)}, /*index=5*/f32[1024,128]{1,0:T(8,128)S(1)}) custom-call(bf16[256,512]{1,0:T(8,128)(2,1)S(1)} %copy-done.1, ...), custom_call_target="tpu_custom_call", output_to_operand_aliasing={{0}: (3, {}), {1}: (4, {}), {2}: (5, {}), {3}: (6, {}), {4}... | custom-call | flops 4294967296 | bytes 65536 | tf_op jit(solution)/shard_map/attend/pallas_call | solution.py:172
  34.4 3.4 %attend.15 = (f32[1024,128]{1,0:T(8,128)S(1)}, f32[1024,128]{1,0:T(8,128)S(1)}, f32[1024,128]{1,0:T(8,128)S(1)}, f32[1024,128]{1,0:T(8,128)S(1)}, f32[1024,128]{1,0:T(8,128)S(1)}, /*index=5*/f32[1024,128]{1,0:T(8,128)S(1)}) custom-call(bf16[256,512]{1,0:T(8,128)(2,1)S(1)} %copy-done.1, ...), custom_call_target="tpu_custom_call", output_to_operand_aliasing={{0}: (3, {}), {1}: (4, {}), {2}: (5, {}), {3}: (6, {}), {4}... | custom-call | flops 4294967296 | bytes 65536 | tf_op jit(solution)/shard_map/attend/pallas_call | solution.py:172
  37.8 1.4 %collective-permute-done.7.refs_2_ = bf16[1024,256]{1,0:T(8,128)(2,1)S(1)} collective-permute-done((bf16[1024,256]{1,0:T(8,128)(2,1)S(1)}, bf16[1024,256]{1,0:T(8,128)(2,1)S(1)}, u32[]{:S(2)}, u32[]{:S(2)}) %collective-permute-start.7) | collective-permute-done | bytes 524320 | tf_op jit(solution)/shard_map/ppermute | solution.py:327
  39.4 3.4 %attend.16 = (f32[1024,128]{1,0:T(8,128)S(1)}, f32[1024,128]{1,0:T(8,128)S(1)}, f32[1024,128]{1,0:T(8,128)S(1)}, f32[1024,128]{1,0:T(8,128)S(1)}, f32[1024,128]{1,0:T(8,128)S(1)}, /*index=5*/f32[1024,128]{1,0:T(8,128)S(1)}) custom-call(bf16[256,512]{1,0:T(8,128)(2,1)S(1)} %copy-done.1, ...), custom_call_target="tpu_custom_call", output_to_operand_aliasing={{0}: (3, {}), {1}: (4, {}), {2}: (5, {}), {3}: (6, {}), {4}... | custom-call | flops 4294967296 | bytes 65536 | tf_op jit(solution)/shard_map/attend/pallas_call | solution.py:172
  42.8 2.8 %collective-permute-done.9.refs_2_ = bf16[1024,256]{1,0:T(8,128)(2,1)S(1)} collective-permute-done((bf16[1024,256]{1,0:T(8,128)(2,1)S(1)}, bf16[1024,256]{1,0:T(8,128)(2,1)S(1)}, u32[]{:S(2)}, u32[]{:S(2)}) %collective-permute-start.9) | collective-permute-done | bytes 524320 | tf_op jit(solution)/shard_map/ppermute | solution.py:325
  45.6 1.3 %collective-permute-done.10.refs_3_ = bf16[512,256]{1,0:T(8,128)(2,1)S(1)} collective-permute-done((bf16[512,256]{1,0:T(8,128)(2,1)S(1)}, bf16[512,256]{1,0:T(8,128)(2,1)S(1)}, u32[]{:S(2)}, u32[]{:S(2)}) %collective-permute-start.10) | collective-permute-done | bytes 262176 | tf_op jit(solution)/shard_map/ppermute | solution.py:327
  48.2 1.5 %collective-permute-start.16 = (bf16[512,1024]{1,0:T(8,128)(2,1)S(1)}, bf16[512,1024]{1,0:T(8,128)(2,1)S(1)}, u32[]{:S(2)}, u32[]{:S(2)}) collective-permute-start(bf16[512,1024]{1,0:T(8,128)(2,1)S(1)} %collective-permute-done.8), channel_id=1, source_target_pairs={{0,1},{1,2},{2,3},{3,0},{8,11},{9,8},{10,9},{11,10},{4,5},{5,6},{6... | collective-permute-start | bytes 3145736 | tf_op jit(solution)/shard_map/ppermute | solution.py:328
  49.7 4.6 %attend.17 = (f32[1024,128]{1,0:T(8,128)S(1)}, f32[1024,128]{1,0:T(8,128)S(1)}, f32[1024,128]{1,0:T(8,128)S(1)}, f32[1024,128]{1,0:T(8,128)S(1)}, f32[1024,128]{1,0:T(8,128)S(1)}, /*index=5*/f32[1024,128]{1,0:T(8,128)S(1)}) custom-call(bf16[256,512]{1,0:T(8,128)(2,1)S(1)} %copy-done.1, ...), custom_call_target="tpu_custom_call", output_to_operand_aliasing={{0}: (4, {}), {1}: (5, {}), {2}: (6, {}), {3}: (7, {}), {4}... | custom-call | flops 2415919104 | bytes 65536 | tf_op jit(solution)/shard_map/attend/pallas_call | solution.py:172
  54.4 1.8 %collective-permute-done.12.refs_2_ = bf16[512,256]{1,0:T(8,128)(2,1)S(1)} collective-permute-done((bf16[512,256]{1,0:T(8,128)(2,1)S(1)}, bf16[512,256]{1,0:T(8,128)(2,1)S(1)}, u32[]{:S(2)}, u32[]{:S(2)}) %collective-permute-start.12) | collective-permute-done | bytes 262176 | tf_op jit(solution)/shard_map/ppermute | solution.py:325
  57.3 2.5 %attend.18 = (f32[1024,128]{1,0:T(8,128)S(1)}, f32[1024,128]{1,0:T(8,128)S(1)}, f32[1024,128]{1,0:T(8,128)S(1)}) custom-call(bf16[256,512]{1,0:T(8,128)(2,1)S(1)} %collective-permute-done.refs_0_.refs_1_, bf16[1024,256]{1,0:T(8,128)(2,1)S(1)} %collective-permute-done.11.refs_1_, ...), custom_call_target="tpu_custom_call", output_to_operand_aliasing={{0}: (3, {}), {1}: (4, {}), {2}: (5, {})} | custom-call | flops 3221225472 | bytes 65536 | tf_op jit(solution)/shard_map/attend/pallas_call | solution.py:172
  60.9 2.5 %attend.19 = (f32[1024,128]{1,0:T(8,128)S(1)}, f32[1024,128]{1,0:T(8,128)S(1)}, f32[1024,128]{1,0:T(8,128)S(1)}) custom-call(bf16[256,512]{1,0:T(8,128)(2,1)S(1)} %copy-done.1, bf16[1024,256]{1,0:T(8,128)(2,1)S(1)} %collective-permute-done.11.refs_1_, ...), custom_call_target="tpu_custom_call", output_to_operand_aliasing={{0}: (3, {}), {1}: (4, {}), {2}: (5, {})} | custom-call | flops 3221225472 | bytes 65536 | tf_op jit(solution)/shard_map/attend/pallas_call | solution.py:172
  64.4 2.3 %collective-permute-done.16.w_mine = bf16[512,1024]{1,0:T(8,128)(2,1)S(1)} collective-permute-done((bf16[512,1024]{1,0:T(8,128)(2,1)S(1)}, bf16[512,1024]{1,0:T(8,128)(2,1)S(1)}, u32[]{:S(2)}, u32[]{:S(2)}) %collective-permute-start.16) | collective-permute-done | bytes 1048608 | tf_op jit(solution)/shard_map/ppermute | solution.py:328
  67.0 3.0 %collective-permute-start.18 = (bf16[128,512]{1,0:T(8,128)(2,1)S(1)}, bf16[128,512]{1,0:T(8,128)(2,1)S(1)}, u32[]{:S(2)}, u32[]{:S(2)}) collective-permute-start(bf16[128,512]{1,0:T(8,128)(2,1)S(1)} %get-tuple-element.256.own), channel_id=1, source_target_pairs={{0,3},{1,0},{2,1},{3,2},{8,9},{9,10},{10,11},{11,8},{4,7},{5,4},{6... | collective-permute-start | bytes 393224 | tf_op jit(solution)/shard_map/ppermute | solution.py:329
  70.5 3.0 %collective-permute-done.17.first = bf16[128,512]{1,0:T(8,128)(2,1)S(1)} collective-permute-done((bf16[128,512]{1,0:T(8,128)(2,1)S(1)}, bf16[128,512]{1,0:T(8,128)(2,1)S(1)}, u32[]{:S(2)}, u32[]{:S(2)}) %collective-permute-start.17) | collective-permute-done | bytes 131104 | tf_op jit(solution)/shard_map/ppermute | solution.py:328
  73.5 2.2 %collective-permute-done.18.second = bf16[128,512]{1,0:T(8,128)(2,1)S(1)} collective-permute-done((bf16[128,512]{1,0:T(8,128)(2,1)S(1)}, bf16[128,512]{1,0:T(8,128)(2,1)S(1)}, u32[]{:S(2)}, u32[]{:S(2)}) %collective-permute-start.18) | collective-permute-done | bytes 131104 | tf_op jit(solution)/shard_map/ppermute | solution.py:329
  75.7 3.8 %collective-permute-start.23 = (bf16[128,512]{1,0:T(8,128)(2,1)S(1)}, bf16[128,512]{1,0:T(8,128)(2,1)S(1)}, u32[]{:S(2)}, u32[]{:S(2)}) collective-permute-start(bf16[128,512]{1,0:T(8,128)(2,1)S(1)} %get-tuple-element.260.own), channel_id=1, source_target_pairs={{0,3},{1,0},{2,1},{3,2},{8,9},{9,10},{10,11},{11,8},{4,7},{5,4},{6... | collective-permute-start | bytes 393224 | tf_op jit(solution)/shard_map/ppermute | solution.py:329
  80.3 1.4 %collective-permute-start.25 = (bf16[128,1024]{1,0:T(8,128)(2,1)S(1)}, bf16[128,1024]{1,0:T(8,128)(2,1)S(1)}, u32[]{:S(2)}, u32[]{:S(2)}) collective-permute-start(bf16[128,1024]{1,0:T(8,128)(2,1)S(1)} %project.6), channel_id=1, source_target_pairs={{0,4},{4,0},{1,5},{5,1},{2,6},{6,2},{3,7},{7,3},{8,12},{12,8},{9,1... | collective-permute-start | bytes 786440 | tf_op jit(solution)/shard_map/ppermute | solution.py:326
  81.7 3.0 %collective-permute-done.23.second = bf16[128,512]{1,0:T(8,128)(2,1)S(1)} collective-permute-done((bf16[128,512]{1,0:T(8,128)(2,1)S(1)}, bf16[128,512]{1,0:T(8,128)(2,1)S(1)}, u32[]{:S(2)}, u32[]{:S(2)}) %collective-permute-start.23) | collective-permute-done | bytes 131104 | tf_op jit(solution)/shard_map/ppermute | solution.py:329
  86.7 1.4 %collective-permute-start.26 = (bf16[128,1024]{1,0:T(8,128)(2,1)S(1)}, bf16[128,1024]{1,0:T(8,128)(2,1)S(1)}, u32[]{:S(2)}, u32[]{:S(2)}) collective-permute-start(bf16[128,1024]{1,0:T(8,128)(2,1)S(1)} %project.7), channel_id=1, source_target_pairs={{0,4},{4,0},{1,5},{5,1},{2,6},{6,2},{3,7},{7,3},{8,12},{12,8},{9,1... | collective-permute-start | bytes 786440 | tf_op jit(solution)/shard_map/ppermute | solution.py:326
  89.7 3.5 %collective-permute-done.26 = bf16[128,1024]{1,0:T(8,128)(2,1)S(1)} collective-permute-done((bf16[128,1024]{1,0:T(8,128)(2,1)S(1)}, bf16[128,1024]{1,0:T(8,128)(2,1)S(1)}, u32[]{:S(2)}, u32[]{:S(2)}) %collective-permute-start.26) | collective-permute-done | bytes 262176 | tf_op jit(solution)/shard_map/ppermute | solution.py:326
  (52 shorter events, 14.6 us)
Async XLA Ops:
  0.0 11.6 %copy-start.1 = (bf16[256,512]{1,0:T(8,128)(2,1)S(1)}, bf16[256,512]{1,0:T(8,128)(2,1)}, u32[]{:S(2)}) copy-start(bf16[256,512]{1,0:T(8,128)(2,1)} %refs_0_.15) | copy-start | bytes 786436
  0.0 11.7 %copy-start = (s32[4]{0:T(128)S(1)}, s32[4]{0:T(128)}, u32[]{:S(2)}) copy-start(s32[4]{0:T(128)} %lengths.1) | copy-start | bytes 52
  0.0 11.7 %copy-start.2 = (bf16[256,128]{1,0:T(8,128)(2,1)S(1)}, bf16[256,128]{1,0:T(8,128)(2,1)}, u32[]{:S(2)}) copy-start(bf16[256,128]{1,0:T(8,128)(2,1)} %refs_1_.1) | copy-start | bytes 196612
  0.0 11.7 %copy-start.3 = (bf16[256,128]{1,0:T(8,128)(2,1)S(1)}, bf16[256,128]{1,0:T(8,128)(2,1)}, u32[]{:S(2)}) copy-start(bf16[256,128]{1,0:T(8,128)(2,1)} %refs_2_.1) | copy-start | bytes 196612
  0.0 1.6 %collective-permute-start.1 = (bf16[512,128]{1,0:T(8,128)(2,1)}, bf16[512,128]{1,0:T(8,128)(2,1)S(1)}, u32[]{:S(2)}, u32[]{:S(2)}) collective-permute-start(bf16[512,128]{1,0:T(8,128)(2,1)} %param.10), channel_id=1, source_target_pairs={{0,8},{8,0},{1,9},{9,1},{2,10},{10,2},{3,11},{11,3},{4,12},{12,4},... | collective-permute-start | bytes 393224 | tf_op jit(solution)/shard_map/ppermute | solution.py:324
  0.1 1.7 %collective-permute-start.2 = (bf16[512,128]{1,0:T(8,128)(2,1)}, bf16[512,128]{1,0:T(8,128)(2,1)S(1)}, u32[]{:S(2)}, u32[]{:S(2)}) collective-permute-start(bf16[512,128]{1,0:T(8,128)(2,1)} %param.11), channel_id=1, source_target_pairs={{0,8},{8,0},{1,9},{9,1},{2,10},{10,2},{3,11},{11,3},{4,12},{12,4},... | collective-permute-start | bytes 393224 | tf_op jit(solution)/shard_map/ppermute | solution.py:324
  1.9 16.6 %collective-permute-start.3 = (bf16[1024,256]{1,0:T(8,128)(2,1)S(1)}, bf16[1024,256]{1,0:T(8,128)(2,1)S(1)}, u32[]{:S(2)}, u32[]{:S(2)}) collective-permute-start(bf16[1024,256]{1,0:T(8,128)(2,1)S(1)} %maximum_maximum_fusion.refs_1_.refs_4_), channel_id=1, source_target_pairs={{0,32},{8,232},{32,64},{40,8},{64,96},{72,40},{96,128},{104,72},{1... | collective-permute-start | bytes 1572872 | tf_op jit(solution)/shard_map/ppermute | solution.py:327
  3.9 6.4 %collective-permute-start = (bf16[256,512]{1,0:T(8,128)(2,1)}, bf16[256,512]{1,0:T(8,128)(2,1)S(1)}, u32[]{:S(2)}, u32[]{:S(2)}) collective-permute-start(bf16[256,512]{1,0:T(8,128)(2,1)} %refs_0_.15), channel_id=1, source_target_pairs={{0,8},{8,0},{1,9},{9,1},{2,10},{10,2},{3,11},{11,3},{4,12},{12,4},... | collective-permute-start | bytes 786440 | tf_op jit(solution)/shard_map/ppermute | solution.py:324
  7.9 15.3 %collective-permute-start.4 = (bf16[512,256]{1,0:T(8,128)(2,1)S(1)}, bf16[512,256]{1,0:T(8,128)(2,1)S(1)}, u32[]{:S(2)}, u32[]{:S(2)}) collective-permute-start(bf16[512,256]{1,0:T(8,128)(2,1)S(1)} %pad_maximum_fusion), channel_id=1, source_target_pairs={{0,16},{16,0},{1,17},{17,1},{2,18},{18,2},{3,19},{19,3},{4,20},{20... | collective-permute-start | bytes 786440 | tf_op jit(solution)/shard_map/ppermute | solution.py:325
  16.9 20.9 %collective-permute-start.8 = (bf16[512,1024]{1,0:T(8,128)(2,1)S(1)}, bf16[512,1024]{1,0:T(8,128)(2,1)S(1)}, u32[]{:S(2)}, u32[]{:S(2)}) collective-permute-start(bf16[512,1024]{1,0:T(8,128)(2,1)S(1)} %get-tuple-element.203), channel_id=1, source_target_pairs={{0,1},{1,2},{2,3},{3,0},{8,11},{9,8},{10,9},{11,10},{4,5},{5,6},{6... | collective-permute-start | bytes 3145736 | tf_op jit(solution)/shard_map/ppermute | solution.py:328
  18.5 10.4 %collective-permute-start.5 = (bf16[1024,256]{1,0:T(8,128)(2,1)S(1)}, bf16[1024,256]{1,0:T(8,128)(2,1)S(1)}, u32[]{:S(2)}, u32[]{:S(2)}) collective-permute-start(bf16[1024,256]{1,0:T(8,128)(2,1)S(1)} %collective-permute-done.3.refs_2_), channel_id=1, source_target_pairs={{0,32},{8,232},{32,64},{40,8},{64,96},{72,40},{96,128},{104,72},{1... | collective-permute-start | bytes 1572872 | tf_op jit(solution)/shard_map/ppermute | solution.py:327
  18.5 15.9 %collective-permute-start.6 = (bf16[1024,256]{1,0:T(8,128)(2,1)S(1)}, bf16[1024,256]{1,0:T(8,128)(2,1)S(1)}, u32[]{:S(2)}, u32[]{:S(2)}) collective-permute-start(bf16[1024,256]{1,0:T(8,128)(2,1)S(1)} %collective-permute-done.3.refs_2_), channel_id=1, source_target_pairs={{0,16},{16,0},{1,17},{17,1},{2,18},{18,2},{3,19},{19,3},{4,20},{20... | collective-permute-start | bytes 1572872 | tf_op jit(solution)/shard_map/ppermute | solution.py:325
  23.2 34.1 %collective-permute-start.13 = (bf16[1024,1024]{1,0:T(8,128)(2,1)S(1)}, bf16[1024,1024]{1,0:T(8,128)(2,1)S(1)}, u32[]{:S(2)}, u32[]{:S(2)}) collective-permute-start(bf16[1024,1024]{1,0:T(8,128)(2,1)S(1)} %get-tuple-element.231), channel_id=1, source_target_pairs={{0,1},{1,2},{2,3},{3,0},{8,11},{9,8},{10,9},{11,10},{4,5},{5,6},{6... | collective-permute-start | bytes 6291464 | tf_op jit(solution)/shard_map/ppermute | solution.py:328
  28.9 10.4 %collective-permute-start.7 = (bf16[1024,256]{1,0:T(8,128)(2,1)S(1)}, bf16[1024,256]{1,0:T(8,128)(2,1)S(1)}, u32[]{:S(2)}, u32[]{:S(2)}) collective-permute-start(bf16[1024,256]{1,0:T(8,128)(2,1)S(1)} %collective-permute-done.5.refs_2_), channel_id=1, source_target_pairs={{0,32},{8,232},{32,64},{40,8},{64,96},{72,40},{96,128},{104,72},{1... | collective-permute-start | bytes 1572872 | tf_op jit(solution)/shard_map/ppermute | solution.py:327
  28.9 16.8 %collective-permute-start.9 = (bf16[1024,256]{1,0:T(8,128)(2,1)S(1)}, bf16[1024,256]{1,0:T(8,128)(2,1)S(1)}, u32[]{:S(2)}, u32[]{:S(2)}) collective-permute-start(bf16[1024,256]{1,0:T(8,128)(2,1)S(1)} %collective-permute-done.5.refs_2_), channel_id=1, source_target_pairs={{0,16},{16,0},{1,17},{17,1},{2,18},{18,2},{3,19},{19,3},{4,20},{20... | collective-permute-start | bytes 1572872 | tf_op jit(solution)/shard_map/ppermute | solution.py:325
  39.3 7.7 %collective-permute-start.10 = (bf16[512,256]{1,0:T(8,128)(2,1)S(1)}, bf16[512,256]{1,0:T(8,128)(2,1)S(1)}, u32[]{:S(2)}, u32[]{:S(2)}) collective-permute-start(bf16[512,256]{1,0:T(8,128)(2,1)S(1)} %slice.3), channel_id=1, source_target_pairs={{0,32},{8,232},{32,64},{40,8},{64,96},{72,40},{96,128},{104,72},{1... | collective-permute-start | bytes 786440 | tf_op jit(solution)/shard_map/ppermute | solution.py:327
  46.9 10.4 %collective-permute-start.11 = (bf16[1024,256]{1,0:T(8,128)(2,1)S(1)}, bf16[1024,256]{1,0:T(8,128)(2,1)S(1)}, u32[]{:S(2)}, u32[]{:S(2)}) collective-permute-start(bf16[1024,256]{1,0:T(8,128)(2,1)S(1)} %collective-permute-done.9.refs_2_), channel_id=1, source_target_pairs={{0,32},{8,232},{32,64},{40,8},{64,96},{72,40},{96,128},{104,72},{1... | collective-permute-start | bytes 1572872 | tf_op jit(solution)/shard_map/ppermute | solution.py:327
  47.0 9.2 %collective-permute-start.12 = (bf16[512,256]{1,0:T(8,128)(2,1)S(1)}, bf16[512,256]{1,0:T(8,128)(2,1)S(1)}, u32[]{:S(2)}, u32[]{:S(2)}) collective-permute-start(bf16[512,256]{1,0:T(8,128)(2,1)S(1)} %collective-permute-done.10.refs_3_), channel_id=1, source_target_pairs={{0,16},{16,0},{1,17},{17,1},{2,18},{18,2},{3,19},{19,3},{4,20},{20... | collective-permute-start | bytes 786440 | tf_op jit(solution)/shard_map/ppermute | solution.py:325
  48.2 18.5 %collective-permute-start.16 = (bf16[512,1024]{1,0:T(8,128)(2,1)S(1)}, bf16[512,1024]{1,0:T(8,128)(2,1)S(1)}, u32[]{:S(2)}, u32[]{:S(2)}) collective-permute-start(bf16[512,1024]{1,0:T(8,128)(2,1)S(1)} %collective-permute-done.8), channel_id=1, source_target_pairs={{0,1},{1,2},{2,3},{3,0},{8,11},{9,8},{10,9},{11,10},{4,5},{5,6},{6... | collective-permute-start | bytes 3145736 | tf_op jit(solution)/shard_map/ppermute | solution.py:328
  57.3 22.2 %collective-permute-start.20 = (bf16[1024,1024]{1,0:T(8,128)(2,1)S(1)}, bf16[1024,1024]{1,0:T(8,128)(2,1)S(1)}, u32[]{:S(2)}, u32[]{:S(2)}) collective-permute-start(bf16[1024,1024]{1,0:T(8,128)(2,1)S(1)} %collective-permute-done.13.w_first), channel_id=1, source_target_pairs={{0,8},{8,0},{1,9},{9,1},{2,10},{10,2},{3,11},{11,3},{4,12},{12,4},... | collective-permute-start | bytes 6291464 | tf_op jit(solution)/shard_map/ppermute | solution.py:324
  60.0 3.4 %collective-permute-start.14 = (bf16[256,512]{1,0:T(8,128)(2,1)S(1)}, bf16[256,512]{1,0:T(8,128)(2,1)S(1)}, u32[]{:S(2)}, u32[]{:S(2)}) collective-permute-start(bf16[256,512]{1,0:T(8,128)(2,1)S(1)} %get-tuple-element.251), channel_id=1, source_target_pairs={{0,8},{8,0},{1,9},{9,1},{2,10},{10,2},{3,11},{11,3},{4,12},{12,4},... | collective-permute-start | bytes 786440 | tf_op jit(solution)/shard_map/ppermute | solution.py:324
  60.6 2.8 %collective-permute-start.15 = (f32[256,128]{1,0:T(8,128)S(1)}, f32[256,128]{1,0:T(8,128)S(1)}, u32[]{:S(2)}, u32[]{:S(2)}) collective-permute-start(f32[256,128]{1,0:T(8,128)S(1)} %get-tuple-element.252), channel_id=1, source_target_pairs={{0,8},{8,0},{1,9},{9,1},{2,10},{10,2},{3,11},{11,3},{4,12},{12,4},... | collective-permute-start | bytes 393224 | tf_op jit(solution)/shard_map/ppermute | solution.py:324
  66.7 12.8 %collective-permute-start.21 = (bf16[512,1024]{1,0:T(8,128)(2,1)S(1)}, bf16[512,1024]{1,0:T(8,128)(2,1)S(1)}, u32[]{:S(2)}, u32[]{:S(2)}) collective-permute-start(bf16[512,1024]{1,0:T(8,128)(2,1)S(1)} %collective-permute-done.16.w_mine), channel_id=1, source_target_pairs={{0,8},{8,0},{1,9},{9,1},{2,10},{10,2},{3,11},{11,3},{4,12},{12,4},... | collective-permute-start | bytes 3145736 | tf_op jit(solution)/shard_map/ppermute | solution.py:324
  66.7 6.8 %collective-permute-start.17 = (bf16[128,512]{1,0:T(8,128)(2,1)S(1)}, bf16[128,512]{1,0:T(8,128)(2,1)S(1)}, u32[]{:S(2)}, u32[]{:S(2)}) collective-permute-start(bf16[128,512]{1,0:T(8,128)(2,1)S(1)} %get-tuple-element.256.own), channel_id=1, source_target_pairs={{0,1},{1,2},{2,3},{3,0},{8,11},{9,8},{10,9},{11,10},{4,5},{5,6},{6... | collective-permute-start | bytes 393224 | tf_op jit(solution)/shard_map/ppermute | solution.py:328
  67.0 8.7 %collective-permute-start.18 = (bf16[128,512]{1,0:T(8,128)(2,1)S(1)}, bf16[128,512]{1,0:T(8,128)(2,1)S(1)}, u32[]{:S(2)}, u32[]{:S(2)}) collective-permute-start(bf16[128,512]{1,0:T(8,128)(2,1)S(1)} %get-tuple-element.256.own), channel_id=1, source_target_pairs={{0,3},{1,0},{2,1},{3,2},{8,9},{9,10},{10,11},{11,8},{4,7},{5,4},{6... | collective-permute-start | bytes 393224 | tf_op jit(solution)/shard_map/ppermute | solution.py:329
  69.9 9.6 %collective-permute-start.19 = (bf16[128,512]{1,0:T(8,128)(2,1)S(1)}, bf16[128,512]{1,0:T(8,128)(2,1)S(1)}, u32[]{:S(2)}, u32[]{:S(2)}) collective-permute-start(bf16[128,512]{1,0:T(8,128)(2,1)S(1)} %get-tuple-element.256.own), channel_id=1, source_target_pairs={{0,2},{1,3},{2,0},{3,1},{4,6},{5,7},{6,4},{7,5},{8,10},{9,11},{10,... | collective-permute-start | bytes 393224 | tf_op jit(solution)/shard_map/ppermute | solution.py:330
  73.5 8.2 %collective-permute-start.22 = (bf16[128,512]{1,0:T(8,128)(2,1)S(1)}, bf16[128,512]{1,0:T(8,128)(2,1)S(1)}, u32[]{:S(2)}, u32[]{:S(2)}) collective-permute-start(bf16[128,512]{1,0:T(8,128)(2,1)S(1)} %get-tuple-element.260.own), channel_id=1, source_target_pairs={{0,1},{1,2},{2,3},{3,0},{8,11},{9,8},{10,9},{11,10},{4,5},{5,6},{6... | collective-permute-start | bytes 393224 | tf_op jit(solution)/shard_map/ppermute | solution.py:328
  75.7 9.1 %collective-permute-start.23 = (bf16[128,512]{1,0:T(8,128)(2,1)S(1)}, bf16[128,512]{1,0:T(8,128)(2,1)S(1)}, u32[]{:S(2)}, u32[]{:S(2)}) collective-permute-start(bf16[128,512]{1,0:T(8,128)(2,1)S(1)} %get-tuple-element.260.own), channel_id=1, source_target_pairs={{0,3},{1,0},{2,1},{3,2},{8,9},{9,10},{10,11},{11,8},{4,7},{5,4},{6... | collective-permute-start | bytes 393224 | tf_op jit(solution)/shard_map/ppermute | solution.py:329
  79.5 6.5 %collective-permute-start.24 = (bf16[128,512]{1,0:T(8,128)(2,1)S(1)}, bf16[128,512]{1,0:T(8,128)(2,1)S(1)}, u32[]{:S(2)}, u32[]{:S(2)}) collective-permute-start(bf16[128,512]{1,0:T(8,128)(2,1)S(1)} %get-tuple-element.260.own), channel_id=1, source_target_pairs={{0,2},{1,3},{2,0},{3,1},{4,6},{5,7},{6,4},{7,5},{8,10},{9,11},{10,... | collective-permute-start | bytes 393224 | tf_op jit(solution)/shard_map/ppermute | solution.py:330
  80.3 9.4 %collective-permute-start.25 = (bf16[128,1024]{1,0:T(8,128)(2,1)S(1)}, bf16[128,1024]{1,0:T(8,128)(2,1)S(1)}, u32[]{:S(2)}, u32[]{:S(2)}) collective-permute-start(bf16[128,1024]{1,0:T(8,128)(2,1)S(1)} %project.6), channel_id=1, source_target_pairs={{0,4},{4,0},{1,5},{5,1},{2,6},{6,2},{3,7},{7,3},{8,12},{12,8},{9,1... | collective-permute-start | bytes 786440 | tf_op jit(solution)/shard_map/ppermute | solution.py:326
  86.7 6.5 %collective-permute-start.26 = (bf16[128,1024]{1,0:T(8,128)(2,1)S(1)}, bf16[128,1024]{1,0:T(8,128)(2,1)S(1)}, u32[]{:S(2)}, u32[]{:S(2)}) collective-permute-start(bf16[128,1024]{1,0:T(8,128)(2,1)S(1)} %project.7), channel_id=1, source_target_pairs={{0,4},{4,0},{1,5},{5,1},{2,6},{6,2},{3,7},{7,3},{8,12},{12,8},{9,1... | collective-permute-start | bytes 786440 | tf_op jit(solution)/shard_map/ppermute | solution.py:326
where the time goes:
time: 95.9 us; the launch traced here: 94.2 us
  Pallas kernels  36 us (38%)
  starting transfers between devices  28.9 us (30%)
  waiting for transfers between devices  26.9 us (28%)
  other arithmetic  2.03 us (2%)
    pallas_call x10, Pallas kernels, attend(): pl.pallas_call(functools.partial(attend_kernel, scale, group, resp_len, s...  28.9 us
    ppermute x2, starting transfers between devices, per_device(): x_back = lambda v: lax.ppermute(v, ('core', 'x'), opposite_x(x_size, -1))  6.79 us
    ppermute x4, starting transfers between devices, per_device(): swap_yh = lambda v: lax.ppermute(v, 'yh', ring(2, 1))  6.15 us
    ppermute x5, waiting for transfers between devices, per_device(): z_hop = lambda v: lax.ppermute(v, ('z', 'core'), opposite(z_size, 1))  5.94 us
    ppermute x7, starting transfers between devices, per_device(): swap_core = lambda v: lax.ppermute(v, 'core', ring(2, 1))  5.48 us
    ppermute x4, waiting for transfers between devices, per_device(): swap_yh = lambda v: lax.ppermute(v, 'yh', ring(2, 1))  5.42 us
    ppermute x5, waiting for transfers between devices, per_device(): x_near = lambda v: lax.ppermute(v, ('core', 'x'), opposite_x(x_size, 1))  5.28 us
    ppermute x2, waiting for transfers between devices, per_device(): x_back = lambda v: lax.ppermute(v, ('core', 'x'), opposite_x(x_size, -1))  5.23 us
  transfers between devices with their start and end apart: 27, of which 14 were waited for; matrix products, arithmetic and copies ran while one was open for 1% of the time, Pallas kernels for 38%

commit v1 on v0

--- a/solution.py
+++ b/solution.py
@@ -277,6 +277,7 @@
         out_shape=shapes,
         scratch_shapes=[pltpu.SemaphoreType.DMA((6,))],
         compiler_params=params(46),
+        cost_estimate=pl.CostEstimate(flops=4096 * 2**20, bytes_accessed=2**20, transcendentals=0),
         name="cut",
     )(places, weight)
 
@@ -359,12 +360,13 @@
         flat, arrays = after((states, arrays))
         return flat, *arrays
 
+    places, pair = after((places, pair))
+    w_near, w_far, w_own = cut(places, out_weight, share)
+    w_far, pair = after((w_far, pair))
+    w_far = x_near(w_far)
     theirs = run([q_core], [(pair, half)], work=8)
     theirs, pair = ordered(theirs, pair)
     states = run([queries], [(pair, half)], None, (lengths, resp_keys, resp_values), work=8) + theirs
-    states, places = ordered(states, places)
-    w_near, w_far, w_own = cut(places, out_weight, share)
-    w_far = x_near(w_far)
     states, a_1 = ordered(states, a_1)
     a_2 = z_hop(a_1)
     b_1 = swap_yh(a_1)
@@ -382,10 +384,11 @@
     w_far = x_near(w_far)
     a_4 = z_hop(a_3[:half])
     states = step(states, (a_3, full))
-    states, b_2, a_4 = ordered(states, b_2, a_4)
+    states, b_2 = ordered(states, b_2)
     b_3 = z_hop(b_2)
+    states, a_4, b_2 = ordered(states, a_4, b_2)
     b_4 = swap_yh(a_4)
-    states = run(query_sets, [(b_2, full), (a_4, half)], states, work=6)
+    states = run(query_sets, [(b_2, full), (a_4, half)], states, work=16)
     states, b_3, b_4, w_near = ordered(states, b_3, b_4, w_near)
     w_back = swap_core(w_near)
     last = [(b_3, full), (b_4, half)]

time: 95.9 us -> 93.1 us (0.971); the launches traced: 94.2 us -> 92.7 us
  waiting for transfers between devices: 26.9 us -> 23.9 us
  starting transfers between devices: 28.9 us -> 31.8 us
  Pallas kernels: 36 us -> 34.6 us
    ppermute x2, starting transfers between devices: 0.6 us -> 5.5 us  [per_device(): x_far = lambda v: lax.ppermute(v, 'x', ring(x_size, 2))]
    ppermute x2, waiting for transfers between devices: 5.23 us -> 0.56 us  [per_device(): x_back = lambda v: lax.ppermute(v, ('core', 'x'), opposite_x(x_size, -1))]
    ppermute x5, waiting for transfers between devices: 5.94 us -> 10.2 us  [per_device(): z_hop = lambda v: lax.ppermute(v, ('z', 'core'), opposite(z_size, 1))]
    ppermute x2, starting transfers between devices: 6.79 us -> 2.87 us  [per_device(): x_back = lambda v: lax.ppermute(v, ('core', 'x'), opposite_x(x_size, -1))]
    ppermute x5, waiting for transfers between devices: 5.28 us -> 2.05 us  [per_device(): x_near = lambda v: lax.ppermute(v, ('core', 'x'), opposite_x(x_size, 1))]
    ppermute x4, waiting for transfers between devices: 5.42 us -> 2.24 us  [per_device(): swap_yh = lambda v: lax.ppermute(v, 'yh', ring(2, 1))]
    ppermute x2, waiting for transfers between devices: 1.24 us -> 3.88 us  [per_device(): x_far = lambda v: lax.ppermute(v, 'x', ring(x_size, 2))]
    pallas_call x10, Pallas kernels: 28.9 us -> 27.5 us  [attend(): pl.pallas_call(functools.partial(attend_kernel, scale, group, resp_len, s...]
  transfers between devices with their start and end apart: 27 -> 27, of which waited for: 14 -> 11; matrix products, arithmetic and copies ran while one was open for 1% -> 1% of each run, Pallas kernels for 38% -> 37%
where the time goes in v1:
time: 93.1 us; the launch traced here: 92.7 us
  Pallas kernels  34.6 us (37%)
  starting transfers between devices  31.8 us (34%)
  waiting for transfers between devices  23.9 us (26%)
  other arithmetic  2.03 us (2%)
    pallas_call x10, Pallas kernels, attend(): pl.pallas_call(functools.partial(attend_kernel, scale, group, resp_len, s...  27.5 us
    ppermute x5, waiting for transfers between devices, per_device(): z_hop = lambda v: lax.ppermute(v, ('z', 'core'), opposite(z_size, 1))  10.2 us
    ppermute x4, starting transfers between devices, per_device(): swap_yh = lambda v: lax.ppermute(v, 'yh', ring(2, 1))  7.15 us
    ppermute x5, starting transfers between devices, per_device(): x_near = lambda v: lax.ppermute(v, ('core', 'x'), opposite_x(x_size, 1))  5.88 us
    ppermute x2, starting transfers between devices, per_device(): x_far = lambda v: lax.ppermute(v, 'x', ring(x_size, 2))  5.5 us
    ppermute x7, starting transfers between devices, per_device(): swap_core = lambda v: lax.ppermute(v, 'core', ring(2, 1))  5.4 us
    ppermute x2, waiting for transfers between devices, per_device(): swap_yl = lambda v: lax.ppermute(v, 'yl', ring(2, 1))  4.71 us
    ppermute x2, waiting for transfers between devices, per_device(): x_far = lambda v: lax.ppermute(v, 'x', ring(x_size, 2))  3.88 us
  transfers between devices with their start and end apart: 27, of which 11 were waited for; matrix products, arithmetic and copies ran while one was open for 1% of the time, Pallas kernels for 37%

profile of v1, /device:TPU:8, one launch (start us, length us, event | category | flops | bytes accessed | tf_op | source)
XLA Modules:
  0.0 92.7 jit_solution(14998449854349915544)
XLA Ops:
  1.8 2.0 %collective-permute-start.3 = (bf16[1024,256]{1,0:T(8,128)(2,1)S(1)}, bf16[1024,256]{1,0:T(8,128)(2,1)S(1)}, u32[]{:S(2)}, u32[]{:S(2)}) collective-permute-start(bf16[1024,256]{1,0:T(8,128)(2,1)S(1)} %maximum_maximum_fusion.refs_1_.refs_4_), channel_id=1, source_target_pairs={{0,32},{8,232},{32,64},{40,8},{64,96},{72,40},{96,128},{104,72},{1... | collective-permute-start | bytes 1572872 | tf_op jit(solution)/shard_map/ppermute | solution.py:328
  3.8 2.3 %collective-permute-start.4 = (bf16[512,256]{1,0:T(8,128)(2,1)S(1)}, bf16[512,256]{1,0:T(8,128)(2,1)S(1)}, u32[]{:S(2)}, u32[]{:S(2)}) collective-permute-start(bf16[512,256]{1,0:T(8,128)(2,1)S(1)} %pad_maximum_fusion), channel_id=1, source_target_pairs={{0,16},{16,0},{1,17},{17,1},{2,18},{18,2},{3,19},{19,3},{4,20},{20... | collective-permute-start | bytes 786440 | tf_op jit(solution)/shard_map/ppermute | solution.py:326
  6.1 3.7 %collective-permute-start = (bf16[256,512]{1,0:T(8,128)(2,1)}, bf16[256,512]{1,0:T(8,128)(2,1)S(1)}, u32[]{:S(2)}, u32[]{:S(2)}) collective-permute-start(bf16[256,512]{1,0:T(8,128)(2,1)} %refs_0_.15), channel_id=1, source_target_pairs={{0,8},{8,0},{1,9},{9,1},{2,10},{10,2},{3,11},{11,3},{4,12},{12,4},... | collective-permute-start | bytes 786440 | tf_op jit(solution)/shard_map/ppermute | solution.py:325
  9.9 3.1 %cut.1 = (bf16[1024,1024]{1,0:T(8,128)(2,1)S(1)}, bf16[512,1024]{1,0:T(8,128)(2,1)S(1)}, bf16[1024,1024]{1,0:T(8,128)(2,1)S(1)}) custom-call(s32[7]{0:T(128)S(1)} %stack.31.places, bf16[512,8192]{1,0:T(8,128)(2,1)} %weight.1), custom_call_target="tpu_custom_call" | custom-call | flops 4294967296 | bytes 1048576 | tf_op jit(solution)/shard_map/cut/pallas_call | solution.py:273
  13.0 1.6 %collective-permute-start.8 = (bf16[512,1024]{1,0:T(8,128)(2,1)S(1)}, bf16[512,1024]{1,0:T(8,128)(2,1)S(1)}, u32[]{:S(2)}, u32[]{:S(2)}) collective-permute-start(bf16[512,1024]{1,0:T(8,128)(2,1)S(1)} %get-tuple-element.204), channel_id=1, source_target_pairs={{0,1},{1,2},{2,3},{3,0},{8,11},{9,8},{10,9},{11,10},{4,5},{5,6},{6... | collective-permute-start | bytes 3145736 | tf_op jit(solution)/shard_map/ppermute | solution.py:329
  14.6 1.4 %attend.10 = (f32[1024,128]{1,0:T(8,128)S(1)}, f32[1024,128]{1,0:T(8,128)S(1)}, f32[1024,128]{1,0:T(8,128)S(1)}) custom-call(bf16[256,512]{1,0:T(8,128)(2,1)S(1)} %collective-permute-done.refs_0_.refs_1_, bf16[1024,256]{1,0:T(8,128)(2,1)S(1)} %maximum_maximum_fusion.refs_1_.refs_4_), custom_call_target="tpu_custom_call" | custom-call | flops 536870912 | bytes 65536 | tf_op jit(solution)/shard_map/attend/pallas_call | solution.py:172
  16.0 2.1 %attend.11 = (f32[1024,128]{1,0:T(8,128)S(1)}, f32[1024,128]{1,0:T(8,128)S(1)}, f32[1024,128]{1,0:T(8,128)S(1)}) custom-call(s32[4]{0:T(128)S(1)} %copy-done, bf16[256,128]{1,0:T(8,128)(2,1)S(1)} %copy-done.2, bf16[256,128]{1,0:T(8,128)(2,1)S(1)} %copy-done.3, bf16[256,512]{1,0:T(8,128)(2,1)S(1)} %copy-done.1, ...), custom_call_target="tpu_custom_call" | custom-call | flops 536870912 | bytes 65536 | tf_op jit(solution)/shard_map/attend/pallas_call | solution.py:172
  18.1 1.3 %collective-permute-start.6 = (bf16[1024,256]{1,0:T(8,128)(2,1)S(1)}, bf16[1024,256]{1,0:T(8,128)(2,1)S(1)}, u32[]{:S(2)}, u32[]{:S(2)}) collective-permute-start(bf16[1024,256]{1,0:T(8,128)(2,1)S(1)} %collective-permute-done.3.refs_2_), channel_id=1, source_target_pairs={{0,16},{16,0},{1,17},{17,1},{2,18},{18,2},{3,19},{19,3},{4,20},{20... | collective-permute-start | bytes 1572872 | tf_op jit(solution)/shard_map/ppermute | solution.py:326
  19.4 3.2 %attend.12 = (f32[1024,128]{1,0:T(8,128)S(1)}, f32[1024,128]{1,0:T(8,128)S(1)}, f32[1024,128]{1,0:T(8,128)S(1)}, f32[1024,128]{1,0:T(8,128)S(1)}, f32[1024,128]{1,0:T(8,128)S(1)}, /*index=5*/f32[1024,128]{1,0:T(8,128)S(1)}) custom-call(bf16[256,512]{1,0:T(8,128)(2,1)S(1)} %copy-done.1, ...), custom_call_target="tpu_custom_call", output_to_operand_aliasing={{0}: (3, {}), {1}: (4, {}), {2}: (5, {}), {3}: (6, {}), {4}... | custom-call | flops 8589934592 | bytes 65536 | tf_op jit(solution)/shard_map/attend/pallas_call | solution.py:172
  22.7 1.6 %collective-permute-start.13 = (bf16[1024,1024]{1,0:T(8,128)(2,1)S(1)}, bf16[1024,1024]{1,0:T(8,128)(2,1)S(1)}, u32[]{:S(2)}, u32[]{:S(2)}) collective-permute-start(bf16[1024,1024]{1,0:T(8,128)(2,1)S(1)} %get-tuple-element.239), channel_id=1, source_target_pairs={{0,1},{1,2},{2,3},{3,0},{8,11},{9,8},{10,9},{11,10},{4,5},{5,6},{6... | collective-permute-start | bytes 6291464 | tf_op jit(solution)/shard_map/ppermute | solution.py:329
  24.2 1.9 %attend.13 = (f32[1024,128]{1,0:T(8,128)S(1)}, f32[1024,128]{1,0:T(8,128)S(1)}, f32[1024,128]{1,0:T(8,128)S(1)}, f32[1024,128]{1,0:T(8,128)S(1)}, f32[1024,128]{1,0:T(8,128)S(1)}, /*index=5*/f32[1024,128]{1,0:T(8,128)S(1)}) custom-call(bf16[256,512]{1,0:T(8,128)(2,1)S(1)} %copy-done.1, ...), custom_call_target="tpu_custom_call", output_to_operand_aliasing={{0}: (3, {}), {1}: (4, {}), {2}: (5, {}), {3}: (6, {}), {4}... | custom-call | flops 4294967296 | bytes 65536 | tf_op jit(solution)/shard_map/attend/pallas_call | solution.py:172
  26.2 3.6 %collective-permute-done.5.refs_2_ = bf16[1024,256]{1,0:T(8,128)(2,1)S(1)} collective-permute-done((bf16[1024,256]{1,0:T(8,128)(2,1)S(1)}, bf16[1024,256]{1,0:T(8,128)(2,1)S(1)}, u32[]{:S(2)}, u32[]{:S(2)}) %collective-permute-start.5) | collective-permute-done | bytes 524320 | tf_op jit(solution)/shard_map/ppermute | solution.py:328
  29.8 2.3 %collective-permute-start.9 = (bf16[1024,256]{1,0:T(8,128)(2,1)S(1)}, bf16[1024,256]{1,0:T(8,128)(2,1)S(1)}, u32[]{:S(2)}, u32[]{:S(2)}) collective-permute-start(bf16[1024,256]{1,0:T(8,128)(2,1)S(1)} %collective-permute-done.5.refs_2_), channel_id=1, source_target_pairs={{0,16},{16,0},{1,17},{17,1},{2,18},{18,2},{3,19},{19,3},{4,20},{20... | collective-permute-start | bytes 1572872 | tf_op jit(solution)/shard_map/ppermute | solution.py:326
  32.1 3.2 %attend.14 = (f32[1024,128]{1,0:T(8,128)S(1)}, f32[1024,128]{1,0:T(8,128)S(1)}, f32[1024,128]{1,0:T(8,128)S(1)}, f32[1024,128]{1,0:T(8,128)S(1)}, f32[1024,128]{1,0:T(8,128)S(1)}, /*index=5*/f32[1024,128]{1,0:T(8,128)S(1)}) custom-call(bf16[256,512]{1,0:T(8,128)(2,1)S(1)} %copy-done.1, ...), custom_call_target="tpu_custom_call", output_to_operand_aliasing={{0}: (3, {}), {1}: (4, {}), {2}: (5, {}), {3}: (6, {}), {4}... | custom-call | flops 4294967296 | bytes 65536 | tf_op jit(solution)/shard_map/attend/pallas_call | solution.py:172
  35.4 3.2 %attend.15 = (f32[1024,128]{1,0:T(8,128)S(1)}, f32[1024,128]{1,0:T(8,128)S(1)}, f32[1024,128]{1,0:T(8,128)S(1)}, f32[1024,128]{1,0:T(8,128)S(1)}, f32[1024,128]{1,0:T(8,128)S(1)}, /*index=5*/f32[1024,128]{1,0:T(8,128)S(1)}) custom-call(bf16[256,512]{1,0:T(8,128)(2,1)S(1)} %copy-done.1, ...), custom_call_target="tpu_custom_call", output_to_operand_aliasing={{0}: (3, {}), {1}: (4, {}), {2}: (5, {}), {3}: (6, {}), {4}... | custom-call | flops 4294967296 | bytes 65536 | tf_op jit(solution)/shard_map/attend/pallas_call | solution.py:172
  38.6 3.9 %collective-permute-done.7.refs_2_ = bf16[1024,256]{1,0:T(8,128)(2,1)S(1)} collective-permute-done((bf16[1024,256]{1,0:T(8,128)(2,1)S(1)}, bf16[1024,256]{1,0:T(8,128)(2,1)S(1)}, u32[]{:S(2)}, u32[]{:S(2)}) %collective-permute-start.7) | collective-permute-done | bytes 524320 | tf_op jit(solution)/shard_map/ppermute | solution.py:328
  42.6 3.2 %attend.16 = (f32[1024,128]{1,0:T(8,128)S(1)}, f32[1024,128]{1,0:T(8,128)S(1)}, f32[1024,128]{1,0:T(8,128)S(1)}, f32[1024,128]{1,0:T(8,128)S(1)}, f32[1024,128]{1,0:T(8,128)S(1)}, /*index=5*/f32[1024,128]{1,0:T(8,128)S(1)}) custom-call(bf16[256,512]{1,0:T(8,128)(2,1)S(1)} %copy-done.1, ...), custom_call_target="tpu_custom_call", output_to_operand_aliasing={{0}: (3, {}), {1}: (4, {}), {2}: (5, {}), {3}: (6, {}), {4}... | custom-call | flops 4294967296 | bytes 65536 | tf_op jit(solution)/shard_map/attend/pallas_call | solution.py:172
  46.0 1.6 %collective-permute-start.16 = (bf16[512,1024]{1,0:T(8,128)(2,1)S(1)}, bf16[512,1024]{1,0:T(8,128)(2,1)S(1)}, u32[]{:S(2)}, u32[]{:S(2)}) collective-permute-start(bf16[512,1024]{1,0:T(8,128)(2,1)S(1)} %collective-permute-done.8), channel_id=1, source_target_pairs={{0,1},{1,2},{2,3},{3,0},{8,11},{9,8},{10,9},{11,10},{4,5},{5,6},{6... | collective-permute-start | bytes 3145736 | tf_op jit(solution)/shard_map/ppermute | solution.py:329
  47.5 2.7 %collective-permute-done.10.refs_3_ = bf16[512,256]{1,0:T(8,128)(2,1)S(1)} collective-permute-done((bf16[512,256]{1,0:T(8,128)(2,1)S(1)}, bf16[512,256]{1,0:T(8,128)(2,1)S(1)}, u32[]{:S(2)}, u32[]{:S(2)}) %collective-permute-start.10) | collective-permute-done | bytes 262176 | tf_op jit(solution)/shard_map/ppermute | solution.py:328
  51.4 4.4 %attend.17 = (f32[1024,128]{1,0:T(8,128)S(1)}, f32[1024,128]{1,0:T(8,128)S(1)}, f32[1024,128]{1,0:T(8,128)S(1)}, f32[1024,128]{1,0:T(8,128)S(1)}, f32[1024,128]{1,0:T(8,128)S(1)}, /*index=5*/f32[1024,128]{1,0:T(8,128)S(1)}) custom-call(bf16[256,512]{1,0:T(8,128)(2,1)S(1)} %copy-done.1, ...), custom_call_target="tpu_custom_call", output_to_operand_aliasing={{0}: (4, {}), {1}: (5, {}), {2}: (6, {}), {3}: (7, {}), {4}... | custom-call | flops 6442450944 | bytes 65536 | tf_op jit(solution)/shard_map/attend/pallas_call | solution.py:172
  55.8 2.2 %collective-permute-done.12.refs_2_ = bf16[512,256]{1,0:T(8,128)(2,1)S(1)} collective-permute-done((bf16[512,256]{1,0:T(8,128)(2,1)S(1)}, bf16[512,256]{1,0:T(8,128)(2,1)S(1)}, u32[]{:S(2)}, u32[]{:S(2)}) %collective-permute-start.12) | collective-permute-done | bytes 262176 | tf_op jit(solution)/shard_map/ppermute | solution.py:326
  58.1 2.4 %attend.18 = (f32[1024,128]{1,0:T(8,128)S(1)}, f32[1024,128]{1,0:T(8,128)S(1)}, f32[1024,128]{1,0:T(8,128)S(1)}) custom-call(bf16[256,512]{1,0:T(8,128)(2,1)S(1)} %collective-permute-done.refs_0_.refs_1_, bf16[1024,256]{1,0:T(8,128)(2,1)S(1)} %collective-permute-done.11.refs_1_, ...), custom_call_target="tpu_custom_call", output_to_operand_aliasing={{0}: (3, {}), {1}: (4, {}), {2}: (5, {})} | custom-call | flops 3221225472 | bytes 65536 | tf_op jit(solution)/shard_map/attend/pallas_call | solution.py:172
  61.5 2.4 %attend.19 = (f32[1024,128]{1,0:T(8,128)S(1)}, f32[1024,128]{1,0:T(8,128)S(1)}, f32[1024,128]{1,0:T(8,128)S(1)}) custom-call(bf16[256,512]{1,0:T(8,128)(2,1)S(1)} %copy-done.1, bf16[1024,256]{1,0:T(8,128)(2,1)S(1)} %collective-permute-done.11.refs_1_, ...), custom_call_target="tpu_custom_call", output_to_operand_aliasing={{0}: (3, {}), {1}: (4, {}), {2}: (5, {})} | custom-call | flops 3221225472 | bytes 65536 | tf_op jit(solution)/shard_map/attend/pallas_call | solution.py:172
  65.2 2.7 %collective-permute-start.19 = (bf16[128,512]{1,0:T(8,128)(2,1)S(1)}, bf16[128,512]{1,0:T(8,128)(2,1)S(1)}, u32[]{:S(2)}, u32[]{:S(2)}) collective-permute-start(bf16[128,512]{1,0:T(8,128)(2,1)S(1)} %get-tuple-element.264.own), channel_id=1, source_target_pairs={{0,2},{1,3},{2,0},{3,1},{4,6},{5,7},{6,4},{7,5},{8,10},{9,11},{10,... | collective-permute-start | bytes 393224 | tf_op jit(solution)/shard_map/ppermute | solution.py:331
  67.9 1.4 %collective-permute-start.18 = (bf16[128,512]{1,0:T(8,128)(2,1)S(1)}, bf16[128,512]{1,0:T(8,128)(2,1)S(1)}, u32[]{:S(2)}, u32[]{:S(2)}) collective-permute-start(bf16[128,512]{1,0:T(8,128)(2,1)S(1)} %get-tuple-element.264.own), channel_id=1, source_target_pairs={{0,3},{1,0},{2,1},{3,2},{8,9},{9,10},{10,11},{11,8},{4,7},{5,4},{6... | collective-permute-start | bytes 393224 | tf_op jit(solution)/shard_map/ppermute | solution.py:330
  69.9 3.1 %collective-permute-done.19.far = bf16[128,512]{1,0:T(8,128)(2,1)S(1)} collective-permute-done((bf16[128,512]{1,0:T(8,128)(2,1)S(1)}, bf16[128,512]{1,0:T(8,128)(2,1)S(1)}, u32[]{:S(2)}, u32[]{:S(2)}) %collective-permute-start.19) | collective-permute-done | bytes 131104 | tf_op jit(solution)/shard_map/ppermute | solution.py:331
  73.0 2.8 %collective-permute-start.24 = (bf16[128,512]{1,0:T(8,128)(2,1)S(1)}, bf16[128,512]{1,0:T(8,128)(2,1)S(1)}, u32[]{:S(2)}, u32[]{:S(2)}) collective-permute-start(bf16[128,512]{1,0:T(8,128)(2,1)S(1)} %get-tuple-element.268.own), channel_id=1, source_target_pairs={{0,2},{1,3},{2,0},{3,1},{4,6},{5,7},{6,4},{7,5},{8,10},{9,11},{10,... | collective-permute-start | bytes 393224 | tf_op jit(solution)/shard_map/ppermute | solution.py:331
  75.8 1.4 %collective-permute-start.23 = (bf16[128,512]{1,0:T(8,128)(2,1)S(1)}, bf16[128,512]{1,0:T(8,128)(2,1)S(1)}, u32[]{:S(2)}, u32[]{:S(2)}) collective-permute-start(bf16[128,512]{1,0:T(8,128)(2,1)S(1)} %get-tuple-element.268.own), channel_id=1, source_target_pairs={{0,3},{1,0},{2,1},{3,2},{8,9},{9,10},{10,11},{11,8},{4,7},{5,4},{6... | collective-permute-start | bytes 393224 | tf_op jit(solution)/shard_map/ppermute | solution.py:330
  78.5 1.4 %collective-permute-start.25 = (bf16[128,1024]{1,0:T(8,128)(2,1)S(1)}, bf16[128,1024]{1,0:T(8,128)(2,1)S(1)}, u32[]{:S(2)}, u32[]{:S(2)}) collective-permute-start(bf16[128,1024]{1,0:T(8,128)(2,1)S(1)} %project.6), channel_id=1, source_target_pairs={{0,4},{4,0},{1,5},{5,1},{2,6},{6,2},{3,7},{7,3},{8,12},{12,8},{9,1... | collective-permute-start | bytes 786440 | tf_op jit(solution)/shard_map/ppermute | solution.py:327
  81.3 2.0 %collective-permute-done.22.first = bf16[128,512]{1,0:T(8,128)(2,1)S(1)} collective-permute-done((bf16[128,512]{1,0:T(8,128)(2,1)S(1)}, bf16[128,512]{1,0:T(8,128)(2,1)S(1)}, u32[]{:S(2)}, u32[]{:S(2)}) %collective-permute-start.22) | collective-permute-done | bytes 131104 | tf_op jit(solution)/shard_map/ppermute | solution.py:329
  84.1 1.4 %collective-permute-start.26 = (bf16[128,1024]{1,0:T(8,128)(2,1)S(1)}, bf16[128,1024]{1,0:T(8,128)(2,1)S(1)}, u32[]{:S(2)}, u32[]{:S(2)}) collective-permute-start(bf16[128,1024]{1,0:T(8,128)(2,1)S(1)} %project.7), channel_id=1, source_target_pairs={{0,4},{4,0},{1,5},{5,1},{2,6},{6,2},{3,7},{7,3},{8,12},{12,8},{9,1... | collective-permute-start | bytes 786440 | tf_op jit(solution)/shard_map/ppermute | solution.py:327
  87.9 3.9 %collective-permute-done.26 = bf16[128,1024]{1,0:T(8,128)(2,1)S(1)} collective-permute-done((bf16[128,1024]{1,0:T(8,128)(2,1)S(1)}, bf16[128,1024]{1,0:T(8,128)(2,1)S(1)}, u32[]{:S(2)}, u32[]{:S(2)}) %collective-permute-start.26) | collective-permute-done | bytes 262176 | tf_op jit(solution)/shard_map/ppermute | solution.py:327
  (52 shorter events, 12.9 us)
Async XLA Ops:
  0.0 1.6 %collective-permute-start.1 = (bf16[512,128]{1,0:T(8,128)(2,1)}, bf16[512,128]{1,0:T(8,128)(2,1)S(1)}, u32[]{:S(2)}, u32[]{:S(2)}) collective-permute-start(bf16[512,128]{1,0:T(8,128)(2,1)} %param.10), channel_id=1, source_target_pairs={{0,8},{8,0},{1,9},{9,1},{2,10},{10,2},{3,11},{11,3},{4,12},{12,4},... | collective-permute-start | bytes 393224 | tf_op jit(solution)/shard_map/ppermute | solution.py:325
  0.0 1.7 %collective-permute-start.2 = (bf16[512,128]{1,0:T(8,128)(2,1)}, bf16[512,128]{1,0:T(8,128)(2,1)S(1)}, u32[]{:S(2)}, u32[]{:S(2)}) collective-permute-start(bf16[512,128]{1,0:T(8,128)(2,1)} %param.11), channel_id=1, source_target_pairs={{0,8},{8,0},{1,9},{9,1},{2,10},{10,2},{3,11},{11,3},{4,12},{12,4},... | collective-permute-start | bytes 393224 | tf_op jit(solution)/shard_map/ppermute | solution.py:325
  1.8 16.3 %collective-permute-start.3 = (bf16[1024,256]{1,0:T(8,128)(2,1)S(1)}, bf16[1024,256]{1,0:T(8,128)(2,1)S(1)}, u32[]{:S(2)}, u32[]{:S(2)}) collective-permute-start(bf16[1024,256]{1,0:T(8,128)(2,1)S(1)} %maximum_maximum_fusion.refs_1_.refs_4_), channel_id=1, source_target_pairs={{0,32},{8,232},{32,64},{40,8},{64,96},{72,40},{96,128},{104,72},{1... | collective-permute-start | bytes 1572872 | tf_op jit(solution)/shard_map/ppermute | solution.py:328
  3.8 18.9 %collective-permute-start.4 = (bf16[512,256]{1,0:T(8,128)(2,1)S(1)}, bf16[512,256]{1,0:T(8,128)(2,1)S(1)}, u32[]{:S(2)}, u32[]{:S(2)}) collective-permute-start(bf16[512,256]{1,0:T(8,128)(2,1)S(1)} %pad_maximum_fusion), channel_id=1, source_target_pairs={{0,16},{16,0},{1,17},{17,1},{2,18},{18,2},{3,19},{19,3},{4,20},{20... | collective-permute-start | bytes 786440 | tf_op jit(solution)/shard_map/ppermute | solution.py:326
  6.1 8.5 %collective-permute-start = (bf16[256,512]{1,0:T(8,128)(2,1)}, bf16[256,512]{1,0:T(8,128)(2,1)S(1)}, u32[]{:S(2)}, u32[]{:S(2)}) collective-permute-start(bf16[256,512]{1,0:T(8,128)(2,1)} %refs_0_.15), channel_id=1, source_target_pairs={{0,8},{8,0},{1,9},{9,1},{2,10},{10,2},{3,11},{11,3},{4,12},{12,4},... | collective-permute-start | bytes 786440 | tf_op jit(solution)/shard_map/ppermute | solution.py:325
  9.9 6.1 %copy-start = (s32[4]{0:T(128)S(1)}, s32[4]{0:T(128)}, u32[]{:S(2)}) copy-start(s32[4]{0:T(128)} %lengths.1) | copy-start | bytes 52
  9.9 6.1 %copy-start.1 = (bf16[256,512]{1,0:T(8,128)(2,1)S(1)}, bf16[256,512]{1,0:T(8,128)(2,1)}, u32[]{:S(2)}) copy-start(bf16[256,512]{1,0:T(8,128)(2,1)} %refs_0_.15) | copy-start | bytes 786436
  9.9 6.1 %copy-start.2 = (bf16[256,128]{1,0:T(8,128)(2,1)S(1)}, bf16[256,128]{1,0:T(8,128)(2,1)}, u32[]{:S(2)}) copy-start(bf16[256,128]{1,0:T(8,128)(2,1)} %refs_1_.1) | copy-start | bytes 196612
  9.9 6.1 %copy-start.3 = (bf16[256,128]{1,0:T(8,128)(2,1)S(1)}, bf16[256,128]{1,0:T(8,128)(2,1)}, u32[]{:S(2)}) copy-start(bf16[256,128]{1,0:T(8,128)(2,1)} %refs_2_.1) | copy-start | bytes 196612
  13.0 25.6 %collective-permute-start.8 = (bf16[512,1024]{1,0:T(8,128)(2,1)S(1)}, bf16[512,1024]{1,0:T(8,128)(2,1)S(1)}, u32[]{:S(2)}, u32[]{:S(2)}) collective-permute-start(bf16[512,1024]{1,0:T(8,128)(2,1)S(1)} %get-tuple-element.204), channel_id=1, source_target_pairs={{0,1},{1,2},{2,3},{3,0},{8,11},{9,8},{10,9},{11,10},{4,5},{5,6},{6... | collective-permute-start | bytes 3145736 | tf_op jit(solution)/shard_map/ppermute | solution.py:329
  18.1 17.3 %collective-permute-start.6 = (bf16[1024,256]{1,0:T(8,128)(2,1)S(1)}, bf16[1024,256]{1,0:T(8,128)(2,1)S(1)}, u32[]{:S(2)}, u32[]{:S(2)}) collective-permute-start(bf16[1024,256]{1,0:T(8,128)(2,1)S(1)} %collective-permute-done.3.refs_2_), channel_id=1, source_target_pairs={{0,16},{16,0},{1,17},{17,1},{2,18},{18,2},{3,19},{19,3},{4,20},{20... | collective-permute-start | bytes 1572872 | tf_op jit(solution)/shard_map/ppermute | solution.py:326
  19.4 10.4 %collective-permute-start.5 = (bf16[1024,256]{1,0:T(8,128)(2,1)S(1)}, bf16[1024,256]{1,0:T(8,128)(2,1)S(1)}, u32[]{:S(2)}, u32[]{:S(2)}) collective-permute-start(bf16[1024,256]{1,0:T(8,128)(2,1)S(1)} %collective-permute-done.3.refs_2_), channel_id=1, source_target_pairs={{0,32},{8,232},{32,64},{40,8},{64,96},{72,40},{96,128},{104,72},{1... | collective-permute-start | bytes 1572872 | tf_op jit(solution)/shard_map/ppermute | solution.py:328
  22.7 35.4 %collective-permute-start.13 = (bf16[1024,1024]{1,0:T(8,128)(2,1)S(1)}, bf16[1024,1024]{1,0:T(8,128)(2,1)S(1)}, u32[]{:S(2)}, u32[]{:S(2)}) collective-permute-start(bf16[1024,1024]{1,0:T(8,128)(2,1)S(1)} %get-tuple-element.239), channel_id=1, source_target_pairs={{0,1},{1,2},{2,3},{3,0},{8,11},{9,8},{10,9},{11,10},{4,5},{5,6},{6... | collective-permute-start | bytes 6291464 | tf_op jit(solution)/shard_map/ppermute | solution.py:329
  29.8 16.1 %collective-permute-start.9 = (bf16[1024,256]{1,0:T(8,128)(2,1)S(1)}, bf16[1024,256]{1,0:T(8,128)(2,1)S(1)}, u32[]{:S(2)}, u32[]{:S(2)}) collective-permute-start(bf16[1024,256]{1,0:T(8,128)(2,1)S(1)} %collective-permute-done.5.refs_2_), channel_id=1, source_target_pairs={{0,16},{16,0},{1,17},{17,1},{2,18},{18,2},{3,19},{19,3},{4,20},{20... | collective-permute-start | bytes 1572872 | tf_op jit(solution)/shard_map/ppermute | solution.py:326
  32.1 10.4 %collective-permute-start.7 = (bf16[1024,256]{1,0:T(8,128)(2,1)S(1)}, bf16[1024,256]{1,0:T(8,128)(2,1)S(1)}, u32[]{:S(2)}, u32[]{:S(2)}) collective-permute-start(bf16[1024,256]{1,0:T(8,128)(2,1)S(1)} %collective-permute-done.5.refs_2_), channel_id=1, source_target_pairs={{0,32},{8,232},{32,64},{40,8},{64,96},{72,40},{96,128},{104,72},{1... | collective-permute-start | bytes 1572872 | tf_op jit(solution)/shard_map/ppermute | solution.py:328
  42.5 7.7 %collective-permute-start.10 = (bf16[512,256]{1,0:T(8,128)(2,1)S(1)}, bf16[512,256]{1,0:T(8,128)(2,1)S(1)}, u32[]{:S(2)}, u32[]{:S(2)}) collective-permute-start(bf16[512,256]{1,0:T(8,128)(2,1)S(1)} %slice.3), channel_id=1, source_target_pairs={{0,32},{8,232},{32,64},{40,8},{64,96},{72,40},{96,128},{104,72},{1... | collective-permute-start | bytes 786440 | tf_op jit(solution)/shard_map/ppermute | solution.py:328
  45.9 12.2 %collective-permute-start.11 = (bf16[1024,256]{1,0:T(8,128)(2,1)S(1)}, bf16[1024,256]{1,0:T(8,128)(2,1)S(1)}, u32[]{:S(2)}, u32[]{:S(2)}) collective-permute-start(bf16[1024,256]{1,0:T(8,128)(2,1)S(1)} %collective-permute-done.9.refs_2_), channel_id=1, source_target_pairs={{0,32},{8,232},{32,64},{40,8},{64,96},{72,40},{96,128},{104,72},{1... | collective-permute-start | bytes 1572872 | tf_op jit(solution)/shard_map/ppermute | solution.py:328
  46.0 18.9 %collective-permute-start.16 = (bf16[512,1024]{1,0:T(8,128)(2,1)S(1)}, bf16[512,1024]{1,0:T(8,128)(2,1)S(1)}, u32[]{:S(2)}, u32[]{:S(2)}) collective-permute-start(bf16[512,1024]{1,0:T(8,128)(2,1)S(1)} %collective-permute-done.8), channel_id=1, source_target_pairs={{0,1},{1,2},{2,3},{3,0},{8,11},{9,8},{10,9},{11,10},{4,5},{5,6},{6... | collective-permute-start | bytes 3145736 | tf_op jit(solution)/shard_map/ppermute | solution.py:329
  50.2 7.9 %collective-permute-start.12 = (bf16[512,256]{1,0:T(8,128)(2,1)S(1)}, bf16[512,256]{1,0:T(8,128)(2,1)S(1)}, u32[]{:S(2)}, u32[]{:S(2)}) collective-permute-start(bf16[512,256]{1,0:T(8,128)(2,1)S(1)} %collective-permute-done.10.refs_3_), channel_id=1, source_target_pairs={{0,16},{16,0},{1,17},{17,1},{2,18},{18,2},{3,19},{19,3},{4,20},{20... | collective-permute-start | bytes 786440 | tf_op jit(solution)/shard_map/ppermute | solution.py:326
  58.1 19.7 %collective-permute-start.20 = (bf16[1024,1024]{1,0:T(8,128)(2,1)S(1)}, bf16[1024,1024]{1,0:T(8,128)(2,1)S(1)}, u32[]{:S(2)}, u32[]{:S(2)}) collective-permute-start(bf16[1024,1024]{1,0:T(8,128)(2,1)S(1)} %collective-permute-done.13.w_first), channel_id=1, source_target_pairs={{0,8},{8,0},{1,9},{9,1},{2,10},{10,2},{3,11},{11,3},{4,12},{12,4},... | collective-permute-start | bytes 6291464 | tf_op jit(solution)/shard_map/ppermute | solution.py:325
  60.6 3.3 %collective-permute-start.15 = (f32[256,128]{1,0:T(8,128)S(1)}, f32[256,128]{1,0:T(8,128)S(1)}, u32[]{:S(2)}, u32[]{:S(2)}) collective-permute-start(f32[256,128]{1,0:T(8,128)S(1)} %get-tuple-element.260), channel_id=1, source_target_pairs={{0,8},{8,0},{1,9},{9,1},{2,10},{10,2},{3,11},{11,3},{4,12},{12,4},... | collective-permute-start | bytes 393224 | tf_op jit(solution)/shard_map/ppermute | solution.py:325
  61.2 2.7 %collective-permute-start.14 = (bf16[256,512]{1,0:T(8,128)(2,1)S(1)}, bf16[256,512]{1,0:T(8,128)(2,1)S(1)}, u32[]{:S(2)}, u32[]{:S(2)}) collective-permute-start(bf16[256,512]{1,0:T(8,128)(2,1)S(1)} %get-tuple-element.259), channel_id=1, source_target_pairs={{0,8},{8,0},{1,9},{9,1},{2,10},{10,2},{3,11},{11,3},{4,12},{12,4},... | collective-permute-start | bytes 786440 | tf_op jit(solution)/shard_map/ppermute | solution.py:325
  64.9 12.9 %collective-permute-start.21 = (bf16[512,1024]{1,0:T(8,128)(2,1)S(1)}, bf16[512,1024]{1,0:T(8,128)(2,1)S(1)}, u32[]{:S(2)}, u32[]{:S(2)}) collective-permute-start(bf16[512,1024]{1,0:T(8,128)(2,1)S(1)} %collective-permute-done.16.w_mine), channel_id=1, source_target_pairs={{0,8},{8,0},{1,9},{9,1},{2,10},{10,2},{3,11},{11,3},{4,12},{12,4},... | collective-permute-start | bytes 3145736 | tf_op jit(solution)/shard_map/ppermute | solution.py:325
  65.2 7.8 %collective-permute-start.19 = (bf16[128,512]{1,0:T(8,128)(2,1)S(1)}, bf16[128,512]{1,0:T(8,128)(2,1)S(1)}, u32[]{:S(2)}, u32[]{:S(2)}) collective-permute-start(bf16[128,512]{1,0:T(8,128)(2,1)S(1)} %get-tuple-element.264.own), channel_id=1, source_target_pairs={{0,2},{1,3},{2,0},{3,1},{4,6},{5,7},{6,4},{7,5},{8,10},{9,11},{10,... | collective-permute-start | bytes 393224 | tf_op jit(solution)/shard_map/ppermute | solution.py:331
  67.9 7.9 %collective-permute-start.18 = (bf16[128,512]{1,0:T(8,128)(2,1)S(1)}, bf16[128,512]{1,0:T(8,128)(2,1)S(1)}, u32[]{:S(2)}, u32[]{:S(2)}) collective-permute-start(bf16[128,512]{1,0:T(8,128)(2,1)S(1)} %get-tuple-element.264.own), channel_id=1, source_target_pairs={{0,3},{1,0},{2,1},{3,2},{8,9},{9,10},{10,11},{11,8},{4,7},{5,4},{6... | collective-permute-start | bytes 393224 | tf_op jit(solution)/shard_map/ppermute | solution.py:330
  69.3 7.9 %collective-permute-start.17 = (bf16[128,512]{1,0:T(8,128)(2,1)S(1)}, bf16[128,512]{1,0:T(8,128)(2,1)S(1)}, u32[]{:S(2)}, u32[]{:S(2)}) collective-permute-start(bf16[128,512]{1,0:T(8,128)(2,1)S(1)} %get-tuple-element.264.own), channel_id=1, source_target_pairs={{0,1},{1,2},{2,3},{3,0},{8,11},{9,8},{10,9},{11,10},{4,5},{5,6},{6... | collective-permute-start | bytes 393224 | tf_op jit(solution)/shard_map/ppermute | solution.py:329
  73.0 7.8 %collective-permute-start.24 = (bf16[128,512]{1,0:T(8,128)(2,1)S(1)}, bf16[128,512]{1,0:T(8,128)(2,1)S(1)}, u32[]{:S(2)}, u32[]{:S(2)}) collective-permute-start(bf16[128,512]{1,0:T(8,128)(2,1)S(1)} %get-tuple-element.268.own), channel_id=1, source_target_pairs={{0,2},{1,3},{2,0},{3,1},{4,6},{5,7},{6,4},{7,5},{8,10},{9,11},{10,... | collective-permute-start | bytes 393224 | tf_op jit(solution)/shard_map/ppermute | solution.py:331
  75.8 5.6 %collective-permute-start.23 = (bf16[128,512]{1,0:T(8,128)(2,1)S(1)}, bf16[128,512]{1,0:T(8,128)(2,1)S(1)}, u32[]{:S(2)}, u32[]{:S(2)}) collective-permute-start(bf16[128,512]{1,0:T(8,128)(2,1)S(1)} %get-tuple-element.268.own), channel_id=1, source_target_pairs={{0,3},{1,0},{2,1},{3,2},{8,9},{9,10},{10,11},{11,8},{4,7},{5,4},{6... | collective-permute-start | bytes 393224 | tf_op jit(solution)/shard_map/ppermute | solution.py:330
  77.2 6.2 %collective-permute-start.22 = (bf16[128,512]{1,0:T(8,128)(2,1)S(1)}, bf16[128,512]{1,0:T(8,128)(2,1)S(1)}, u32[]{:S(2)}, u32[]{:S(2)}) collective-permute-start(bf16[128,512]{1,0:T(8,128)(2,1)S(1)} %get-tuple-element.268.own), channel_id=1, source_target_pairs={{0,1},{1,2},{2,3},{3,0},{8,11},{9,8},{10,9},{11,10},{4,5},{5,6},{6... | collective-permute-start | bytes 393224 | tf_op jit(solution)/shard_map/ppermute | solution.py:329
  78.5 9.3 %collective-permute-start.25 = (bf16[128,1024]{1,0:T(8,128)(2,1)S(1)}, bf16[128,1024]{1,0:T(8,128)(2,1)S(1)}, u32[]{:S(2)}, u32[]{:S(2)}) collective-permute-start(bf16[128,1024]{1,0:T(8,128)(2,1)S(1)} %project.6), channel_id=1, source_target_pairs={{0,4},{4,0},{1,5},{5,1},{2,6},{6,2},{3,7},{7,3},{8,12},{12,8},{9,1... | collective-permute-start | bytes 786440 | tf_op jit(solution)/shard_map/ppermute | solution.py:327
  84.1 7.6 %collective-permute-start.26 = (bf16[128,1024]{1,0:T(8,128)(2,1)S(1)}, bf16[128,1024]{1,0:T(8,128)(2,1)S(1)}, u32[]{:S(2)}, u32[]{:S(2)}) collective-permute-start(bf16[128,1024]{1,0:T(8,128)(2,1)S(1)} %project.7), channel_id=1, source_target_pairs={{0,4},{4,0},{1,5},{5,1},{2,6},{6,2},{3,7},{7,3},{8,12},{12,8},{9,1... | collective-permute-start | bytes 786440 | tf_op jit(solution)/shard_map/ppermute | solution.py:327

commit v2 on v1

--- a/solution.py
+++ b/solution.py
@@ -328,7 +328,6 @@
     z_hop = lambda v: lax.ppermute(v, ("z", "core"), opposite(z_size, 1))
     x_near = lambda v: lax.ppermute(v, ("core", "x"), opposite_x(x_size, 1))
     x_back = lambda v: lax.ppermute(v, ("core", "x"), opposite_x(x_size, -1))
-    x_far = lambda v: lax.ppermute(v, "x", ring(x_size, 2))
 
     after = lax.optimization_barrier
 
@@ -401,7 +400,10 @@
 
     attended, w_far = after((attended, w_far))
     w_other = swap_core(w_far)
-    gathered = [[rows, x_near(rows), x_back(rows), x_far(rows)] for rows in attended]
+    gathered = []
+    for rows in attended:
+        near = x_near(rows)
+        gathered.append([rows, near, x_back(rows), x_near(near)])
     weights = [w_own, w_near, w_back, w_far, w_other]
     away = [project(1, core, rows, weights) for rows in gathered]
     arrived = [swap_yl(rows) for rows in away]

time: 93.1 us -> 91.9 us (0.987)
  starting transfers between devices: 31.8 us -> 29.4 us
  waiting for transfers between devices: 23.9 us -> 25.5 us
    ppermute x2 -> x0, starting transfers between devices: 5.5 us -> none  [per_device(): x_far = lambda v: lax.ppermute(v, 'x', ring(x_size, 2))]
    ppermute x5 -> x7, waiting for transfers between devices: 2.05 us -> 7.3 us  [per_device(): x_near = lambda v: lax.ppermute(v, ('core', 'x'), opposite_x(x_size, 1))]
    ppermute x2 -> x0, waiting for transfers between devices: 3.88 us -> none  [per_device(): x_far = lambda v: lax.ppermute(v, 'x', ring(x_size, 2))]
    ppermute x2, starting transfers between devices: 2.87 us -> 4.63 us  [per_device(): x_back = lambda v: lax.ppermute(v, ('core', 'x'), opposite_x(x_size, -1))]
    ppermute x5 -> x7, starting transfers between devices: 5.88 us -> 7.14 us  [per_device(): x_near = lambda v: lax.ppermute(v, ('core', 'x'), opposite_x(x_size, 1))]
  transfers between devices with their start and end apart: 27 -> 27, of which waited for: 11 -> 10; matrix products, arithmetic and copies ran while one was open for 1% -> 1% of each run, Pallas kernels for 37% -> 38%
where the time goes in v2:
time: 91.9 us; the launch traced here: 91.8 us
  Pallas kernels  34.5 us (38%)
  starting transfers between devices  29.4 us (32%)
  waiting for transfers between devices  25.5 us (28%)
  other arithmetic  2.03 us (2%)
    pallas_call x10, Pallas kernels, attend(): pl.pallas_call(functools.partial(attend_kernel, scale, group, resp_len, s...  27.5 us
    ppermute x5, waiting for transfers between devices, per_device(): z_hop = lambda v: lax.ppermute(v, ('z', 'core'), opposite(z_size, 1))  10.2 us
    ppermute x7, waiting for transfers between devices, per_device(): x_near = lambda v: lax.ppermute(v, ('core', 'x'), opposite_x(x_size, 1))  7.3 us
    ppermute x4, starting transfers between devices, per_device(): swap_yh = lambda v: lax.ppermute(v, 'yh', ring(2, 1))  7.15 us
    ppermute x7, starting transfers between devices, per_device(): x_near = lambda v: lax.ppermute(v, ('core', 'x'), opposite_x(x_size, 1))  7.14 us
    ppermute x2, waiting for transfers between devices, per_device(): swap_yl = lambda v: lax.ppermute(v, 'yl', ring(2, 1))  5.54 us
    ppermute x7, starting transfers between devices, per_device(): swap_core = lambda v: lax.ppermute(v, 'core', ring(2, 1))  5.4 us
    ppermute x2, starting transfers between devices, per_device(): x_back = lambda v: lax.ppermute(v, ('core', 'x'), opposite_x(x_size, -1))  4.63 us
  transfers between devices with their start and end apart: 27, of which 10 were waited for; matrix products, arithmetic and copies ran while one was open for 1% of the time, Pallas kernels for 38%

profile of v2, /device:TPU:8, one launch (start us, length us, event | category | flops | bytes accessed | tf_op | source)
XLA Modules:
  0.0 91.8 jit_solution(10570176558100538633)
XLA Ops:
  1.8 2.0 %collective-permute-start.3 = (bf16[1024,256]{1,0:T(8,128)(2,1)S(1)}, bf16[1024,256]{1,0:T(8,128)(2,1)S(1)}, u32[]{:S(2)}, u32[]{:S(2)}) collective-permute-start(bf16[1024,256]{1,0:T(8,128)(2,1)S(1)} %maximum_maximum_fusion.refs_1_.refs_4_), channel_id=1, source_target_pairs={{0,32},{8,232},{32,64},{40,8},{64,96},{72,40},{96,128},{104,72},{1... | collective-permute-start | bytes 1572872 | tf_op jit(solution)/shard_map/ppermute | solution.py:328
  3.8 2.3 %collective-permute-start.4 = (bf16[512,256]{1,0:T(8,128)(2,1)S(1)}, bf16[512,256]{1,0:T(8,128)(2,1)S(1)}, u32[]{:S(2)}, u32[]{:S(2)}) collective-permute-start(bf16[512,256]{1,0:T(8,128)(2,1)S(1)} %pad_maximum_fusion), channel_id=1, source_target_pairs={{0,16},{16,0},{1,17},{17,1},{2,18},{18,2},{3,19},{19,3},{4,20},{20... | collective-permute-start | bytes 786440 | tf_op jit(solution)/shard_map/ppermute | solution.py:326
  6.1 3.7 %collective-permute-start = (bf16[256,512]{1,0:T(8,128)(2,1)}, bf16[256,512]{1,0:T(8,128)(2,1)S(1)}, u32[]{:S(2)}, u32[]{:S(2)}) collective-permute-start(bf16[256,512]{1,0:T(8,128)(2,1)} %refs_0_.15), channel_id=1, source_target_pairs={{0,8},{8,0},{1,9},{9,1},{2,10},{10,2},{3,11},{11,3},{4,12},{12,4},... | collective-permute-start | bytes 786440 | tf_op jit(solution)/shard_map/ppermute | solution.py:325
  9.9 3.1 %cut.1 = (bf16[1024,1024]{1,0:T(8,128)(2,1)S(1)}, bf16[512,1024]{1,0:T(8,128)(2,1)S(1)}, bf16[1024,1024]{1,0:T(8,128)(2,1)S(1)}) custom-call(s32[7]{0:T(128)S(1)} %stack.31.places, bf16[512,8192]{1,0:T(8,128)(2,1)} %weight.1), custom_call_target="tpu_custom_call" | custom-call | flops 4294967296 | bytes 1048576 | tf_op jit(solution)/shard_map/cut/pallas_call | solution.py:273
  13.0 1.6 %collective-permute-start.8 = (bf16[512,1024]{1,0:T(8,128)(2,1)S(1)}, bf16[512,1024]{1,0:T(8,128)(2,1)S(1)}, u32[]{:S(2)}, u32[]{:S(2)}) collective-permute-start(bf16[512,1024]{1,0:T(8,128)(2,1)S(1)} %get-tuple-element.204), channel_id=1, source_target_pairs={{0,1},{1,2},{2,3},{3,0},{8,11},{9,8},{10,9},{11,10},{4,5},{5,6},{6... | collective-permute-start | bytes 3145736 | tf_op jit(solution)/shard_map/ppermute | solution.py:329
  14.6 1.4 %attend.10 = (f32[1024,128]{1,0:T(8,128)S(1)}, f32[1024,128]{1,0:T(8,128)S(1)}, f32[1024,128]{1,0:T(8,128)S(1)}) custom-call(bf16[256,512]{1,0:T(8,128)(2,1)S(1)} %collective-permute-done.refs_0_.refs_1_, bf16[1024,256]{1,0:T(8,128)(2,1)S(1)} %maximum_maximum_fusion.refs_1_.refs_4_), custom_call_target="tpu_custom_call" | custom-call | flops 536870912 | bytes 65536 | tf_op jit(solution)/shard_map/attend/pallas_call | solution.py:172
  16.0 2.1 %attend.11 = (f32[1024,128]{1,0:T(8,128)S(1)}, f32[1024,128]{1,0:T(8,128)S(1)}, f32[1024,128]{1,0:T(8,128)S(1)}) custom-call(s32[4]{0:T(128)S(1)} %copy-done, bf16[256,128]{1,0:T(8,128)(2,1)S(1)} %copy-done.2, bf16[256,128]{1,0:T(8,128)(2,1)S(1)} %copy-done.3, bf16[256,512]{1,0:T(8,128)(2,1)S(1)} %copy-done.1, ...), custom_call_target="tpu_custom_call" | custom-call | flops 536870912 | bytes 65536 | tf_op jit(solution)/shard_map/attend/pallas_call | solution.py:172
  18.1 1.3 %collective-permute-start.6 = (bf16[1024,256]{1,0:T(8,128)(2,1)S(1)}, bf16[1024,256]{1,0:T(8,128)(2,1)S(1)}, u32[]{:S(2)}, u32[]{:S(2)}) collective-permute-start(bf16[1024,256]{1,0:T(8,128)(2,1)S(1)} %collective-permute-done.3.refs_2_), channel_id=1, source_target_pairs={{0,16},{16,0},{1,17},{17,1},{2,18},{18,2},{3,19},{19,3},{4,20},{20... | collective-permute-start | bytes 1572872 | tf_op jit(solution)/shard_map/ppermute | solution.py:326
  19.4 3.2 %attend.12 = (f32[1024,128]{1,0:T(8,128)S(1)}, f32[1024,128]{1,0:T(8,128)S(1)}, f32[1024,128]{1,0:T(8,128)S(1)}, f32[1024,128]{1,0:T(8,128)S(1)}, f32[1024,128]{1,0:T(8,128)S(1)}, /*index=5*/f32[1024,128]{1,0:T(8,128)S(1)}) custom-call(bf16[256,512]{1,0:T(8,128)(2,1)S(1)} %copy-done.1, ...), custom_call_target="tpu_custom_call", output_to_operand_aliasing={{0}: (3, {}), {1}: (4, {}), {2}: (5, {}), {3}: (6, {}), {4}... | custom-call | flops 8589934592 | bytes 65536 | tf_op jit(solution)/shard_map/attend/pallas_call | solution.py:172
  22.7 1.6 %collective-permute-start.13 = (bf16[1024,1024]{1,0:T(8,128)(2,1)S(1)}, bf16[1024,1024]{1,0:T(8,128)(2,1)S(1)}, u32[]{:S(2)}, u32[]{:S(2)}) collective-permute-start(bf16[1024,1024]{1,0:T(8,128)(2,1)S(1)} %get-tuple-element.239), channel_id=1, source_target_pairs={{0,1},{1,2},{2,3},{3,0},{8,11},{9,8},{10,9},{11,10},{4,5},{5,6},{6... | collective-permute-start | bytes 6291464 | tf_op jit(solution)/shard_map/ppermute | solution.py:329
  24.2 1.9 %attend.13 = (f32[1024,128]{1,0:T(8,128)S(1)}, f32[1024,128]{1,0:T(8,128)S(1)}, f32[1024,128]{1,0:T(8,128)S(1)}, f32[1024,128]{1,0:T(8,128)S(1)}, f32[1024,128]{1,0:T(8,128)S(1)}, /*index=5*/f32[1024,128]{1,0:T(8,128)S(1)}) custom-call(bf16[256,512]{1,0:T(8,128)(2,1)S(1)} %copy-done.1, ...), custom_call_target="tpu_custom_call", output_to_operand_aliasing={{0}: (3, {}), {1}: (4, {}), {2}: (5, {}), {3}: (6, {}), {4}... | custom-call | flops 4294967296 | bytes 65536 | tf_op jit(solution)/shard_map/attend/pallas_call | solution.py:172
  26.2 3.6 %collective-permute-done.5.refs_2_ = bf16[1024,256]{1,0:T(8,128)(2,1)S(1)} collective-permute-done((bf16[1024,256]{1,0:T(8,128)(2,1)S(1)}, bf16[1024,256]{1,0:T(8,128)(2,1)S(1)}, u32[]{:S(2)}, u32[]{:S(2)}) %collective-permute-start.5) | collective-permute-done | bytes 524320 | tf_op jit(solution)/shard_map/ppermute | solution.py:328
  29.8 2.3 %collective-permute-start.9 = (bf16[1024,256]{1,0:T(8,128)(2,1)S(1)}, bf16[1024,256]{1,0:T(8,128)(2,1)S(1)}, u32[]{:S(2)}, u32[]{:S(2)}) collective-permute-start(bf16[1024,256]{1,0:T(8,128)(2,1)S(1)} %collective-permute-done.5.refs_2_), channel_id=1, source_target_pairs={{0,16},{16,0},{1,17},{17,1},{2,18},{18,2},{3,19},{19,3},{4,20},{20... | collective-permute-start | bytes 1572872 | tf_op jit(solution)/shard_map/ppermute | solution.py:326
  32.1 3.2 %attend.14 = (f32[1024,128]{1,0:T(8,128)S(1)}, f32[1024,128]{1,0:T(8,128)S(1)}, f32[1024,128]{1,0:T(8,128)S(1)}, f32[1024,128]{1,0:T(8,128)S(1)}, f32[1024,128]{1,0:T(8,128)S(1)}, /*index=5*/f32[1024,128]{1,0:T(8,128)S(1)}) custom-call(bf16[256,512]{1,0:T(8,128)(2,1)S(1)} %copy-done.1, ...), custom_call_target="tpu_custom_call", output_to_operand_aliasing={{0}: (3, {}), {1}: (4, {}), {2}: (5, {}), {3}: (6, {}), {4}... | custom-call | flops 4294967296 | bytes 65536 | tf_op jit(solution)/shard_map/attend/pallas_call | solution.py:172
  35.4 3.2 %attend.15 = (f32[1024,128]{1,0:T(8,128)S(1)}, f32[1024,128]{1,0:T(8,128)S(1)}, f32[1024,128]{1,0:T(8,128)S(1)}, f32[1024,128]{1,0:T(8,128)S(1)}, f32[1024,128]{1,0:T(8,128)S(1)}, /*index=5*/f32[1024,128]{1,0:T(8,128)S(1)}) custom-call(bf16[256,512]{1,0:T(8,128)(2,1)S(1)} %copy-done.1, ...), custom_call_target="tpu_custom_call", output_to_operand_aliasing={{0}: (3, {}), {1}: (4, {}), {2}: (5, {}), {3}: (6, {}), {4}... | custom-call | flops 4294967296 | bytes 65536 | tf_op jit(solution)/shard_map/attend/pallas_call | solution.py:172
  38.6 3.9 %collective-permute-done.7.refs_2_ = bf16[1024,256]{1,0:T(8,128)(2,1)S(1)} collective-permute-done((bf16[1024,256]{1,0:T(8,128)(2,1)S(1)}, bf16[1024,256]{1,0:T(8,128)(2,1)S(1)}, u32[]{:S(2)}, u32[]{:S(2)}) %collective-permute-start.7) | collective-permute-done | bytes 524320 | tf_op jit(solution)/shard_map/ppermute | solution.py:328
  42.6 3.2 %attend.16 = (f32[1024,128]{1,0:T(8,128)S(1)}, f32[1024,128]{1,0:T(8,128)S(1)}, f32[1024,128]{1,0:T(8,128)S(1)}, f32[1024,128]{1,0:T(8,128)S(1)}, f32[1024,128]{1,0:T(8,128)S(1)}, /*index=5*/f32[1024,128]{1,0:T(8,128)S(1)}) custom-call(bf16[256,512]{1,0:T(8,128)(2,1)S(1)} %copy-done.1, ...), custom_call_target="tpu_custom_call", output_to_operand_aliasing={{0}: (3, {}), {1}: (4, {}), {2}: (5, {}), {3}: (6, {}), {4}... | custom-call | flops 4294967296 | bytes 65536 | tf_op jit(solution)/shard_map/attend/pallas_call | solution.py:172
  46.0 1.6 %collective-permute-start.16 = (bf16[512,1024]{1,0:T(8,128)(2,1)S(1)}, bf16[512,1024]{1,0:T(8,128)(2,1)S(1)}, u32[]{:S(2)}, u32[]{:S(2)}) collective-permute-start(bf16[512,1024]{1,0:T(8,128)(2,1)S(1)} %collective-permute-done.8), channel_id=1, source_target_pairs={{0,1},{1,2},{2,3},{3,0},{8,11},{9,8},{10,9},{11,10},{4,5},{5,6},{6... | collective-permute-start | bytes 3145736 | tf_op jit(solution)/shard_map/ppermute | solution.py:329
  47.5 2.7 %collective-permute-done.10.refs_3_ = bf16[512,256]{1,0:T(8,128)(2,1)S(1)} collective-permute-done((bf16[512,256]{1,0:T(8,128)(2,1)S(1)}, bf16[512,256]{1,0:T(8,128)(2,1)S(1)}, u32[]{:S(2)}, u32[]{:S(2)}) %collective-permute-start.10) | collective-permute-done | bytes 262176 | tf_op jit(solution)/shard_map/ppermute | solution.py:328
  51.4 4.4 %attend.17 = (f32[1024,128]{1,0:T(8,128)S(1)}, f32[1024,128]{1,0:T(8,128)S(1)}, f32[1024,128]{1,0:T(8,128)S(1)}, f32[1024,128]{1,0:T(8,128)S(1)}, f32[1024,128]{1,0:T(8,128)S(1)}, /*index=5*/f32[1024,128]{1,0:T(8,128)S(1)}) custom-call(bf16[256,512]{1,0:T(8,128)(2,1)S(1)} %copy-done.1, ...), custom_call_target="tpu_custom_call", output_to_operand_aliasing={{0}: (4, {}), {1}: (5, {}), {2}: (6, {}), {3}: (7, {}), {4}... | custom-call | flops 6442450944 | bytes 65536 | tf_op jit(solution)/shard_map/attend/pallas_call | solution.py:172
  55.8 2.2 %collective-permute-done.12.refs_2_ = bf16[512,256]{1,0:T(8,128)(2,1)S(1)} collective-permute-done((bf16[512,256]{1,0:T(8,128)(2,1)S(1)}, bf16[512,256]{1,0:T(8,128)(2,1)S(1)}, u32[]{:S(2)}, u32[]{:S(2)}) %collective-permute-start.12) | collective-permute-done | bytes 262176 | tf_op jit(solution)/shard_map/ppermute | solution.py:326
  58.1 2.4 %attend.18 = (f32[1024,128]{1,0:T(8,128)S(1)}, f32[1024,128]{1,0:T(8,128)S(1)}, f32[1024,128]{1,0:T(8,128)S(1)}) custom-call(bf16[256,512]{1,0:T(8,128)(2,1)S(1)} %collective-permute-done.refs_0_.refs_1_, bf16[1024,256]{1,0:T(8,128)(2,1)S(1)} %collective-permute-done.11.refs_1_, ...), custom_call_target="tpu_custom_call", output_to_operand_aliasing={{0}: (3, {}), {1}: (4, {}), {2}: (5, {})} | custom-call | flops 3221225472 | bytes 65536 | tf_op jit(solution)/shard_map/attend/pallas_call | solution.py:172
  61.5 2.4 %attend.19 = (f32[1024,128]{1,0:T(8,128)S(1)}, f32[1024,128]{1,0:T(8,128)S(1)}, f32[1024,128]{1,0:T(8,128)S(1)}) custom-call(bf16[256,512]{1,0:T(8,128)(2,1)S(1)} %copy-done.1, bf16[1024,256]{1,0:T(8,128)(2,1)S(1)} %collective-permute-done.11.refs_1_, ...), custom_call_target="tpu_custom_call", output_to_operand_aliasing={{0}: (3, {}), {1}: (4, {}), {2}: (5, {})} | custom-call | flops 3221225472 | bytes 65536 | tf_op jit(solution)/shard_map/attend/pallas_call | solution.py:172
  65.2 1.5 %collective-permute-start.17 = (bf16[128,512]{1,0:T(8,128)(2,1)S(1)}, bf16[128,512]{1,0:T(8,128)(2,1)S(1)}, u32[]{:S(2)}, u32[]{:S(2)}) collective-permute-start(bf16[128,512]{1,0:T(8,128)(2,1)S(1)} %get-tuple-element.264.own), channel_id=1, source_target_pairs={{0,1},{1,2},{2,3},{3,0},{8,11},{9,8},{10,9},{11,10},{4,5},{5,6},{6... | collective-permute-start | bytes 393224 | tf_op jit(solution)/shard_map/ppermute | solution.py:329
  66.6 1.7 %collective-permute-start.18 = (bf16[128,512]{1,0:T(8,128)(2,1)S(1)}, bf16[128,512]{1,0:T(8,128)(2,1)S(1)}, u32[]{:S(2)}, u32[]{:S(2)}) collective-permute-start(bf16[128,512]{1,0:T(8,128)(2,1)S(1)} %get-tuple-element.264.own), channel_id=1, source_target_pairs={{0,3},{1,0},{2,1},{3,2},{8,9},{9,10},{10,11},{11,8},{4,7},{5,4},{6... | collective-permute-start | bytes 393224 | tf_op jit(solution)/shard_map/ppermute | solution.py:330
  68.7 3.3 %collective-permute-done.17.first = bf16[128,512]{1,0:T(8,128)(2,1)S(1)} collective-permute-done((bf16[128,512]{1,0:T(8,128)(2,1)S(1)}, bf16[128,512]{1,0:T(8,128)(2,1)S(1)}, u32[]{:S(2)}, u32[]{:S(2)}) %collective-permute-start.17) | collective-permute-done | bytes 131104 | tf_op jit(solution)/shard_map/ppermute | solution.py:329
  72.6 2.9 %collective-permute-start.23 = (bf16[128,512]{1,0:T(8,128)(2,1)S(1)}, bf16[128,512]{1,0:T(8,128)(2,1)S(1)}, u32[]{:S(2)}, u32[]{:S(2)}) collective-permute-start(bf16[128,512]{1,0:T(8,128)(2,1)S(1)} %get-tuple-element.268.own), channel_id=1, source_target_pairs={{0,3},{1,0},{2,1},{3,2},{8,9},{9,10},{10,11},{11,8},{4,7},{5,4},{6... | collective-permute-start | bytes 393224 | tf_op jit(solution)/shard_map/ppermute | solution.py:330
  75.5 3.7 %collective-permute-done.19.far = bf16[128,512]{1,0:T(8,128)(2,1)S(1)} collective-permute-done((bf16[128,512]{1,0:T(8,128)(2,1)S(1)}, bf16[128,512]{1,0:T(8,128)(2,1)S(1)}, u32[]{:S(2)}, u32[]{:S(2)}) %collective-permute-start.19) | collective-permute-done | bytes 131104 | tf_op jit(solution)/shard_map/ppermute | solution.py:329
  79.9 1.4 %collective-permute-start.25 = (bf16[128,1024]{1,0:T(8,128)(2,1)S(1)}, bf16[128,1024]{1,0:T(8,128)(2,1)S(1)}, u32[]{:S(2)}, u32[]{:S(2)}) collective-permute-start(bf16[128,1024]{1,0:T(8,128)(2,1)S(1)} %project.6), channel_id=1, source_target_pairs={{0,4},{4,0},{1,5},{5,1},{2,6},{6,2},{3,7},{7,3},{8,12},{12,8},{9,1... | collective-permute-start | bytes 786440 | tf_op jit(solution)/shard_map/ppermute | solution.py:327
  82.4 1.4 %collective-permute-start.26 = (bf16[128,1024]{1,0:T(8,128)(2,1)S(1)}, bf16[128,1024]{1,0:T(8,128)(2,1)S(1)}, u32[]{:S(2)}, u32[]{:S(2)}) collective-permute-start(bf16[128,1024]{1,0:T(8,128)(2,1)S(1)} %project.7), channel_id=1, source_target_pairs={{0,4},{4,0},{1,5},{5,1},{2,6},{6,2},{3,7},{7,3},{8,12},{12,8},{9,1... | collective-permute-start | bytes 786440 | tf_op jit(solution)/shard_map/ppermute | solution.py:327
  85.3 2.7 %collective-permute-done.25 = bf16[128,1024]{1,0:T(8,128)(2,1)S(1)} collective-permute-done((bf16[128,1024]{1,0:T(8,128)(2,1)S(1)}, bf16[128,1024]{1,0:T(8,128)(2,1)S(1)}, u32[]{:S(2)}, u32[]{:S(2)}) %collective-permute-start.25) | collective-permute-done | bytes 262176 | tf_op jit(solution)/shard_map/ppermute | solution.py:327
  88.0 2.8 %collective-permute-done.26 = bf16[128,1024]{1,0:T(8,128)(2,1)S(1)} collective-permute-done((bf16[128,1024]{1,0:T(8,128)(2,1)S(1)}, bf16[128,1024]{1,0:T(8,128)(2,1)S(1)}, u32[]{:S(2)}, u32[]{:S(2)}) %collective-permute-start.26) | collective-permute-done | bytes 262176 | tf_op jit(solution)/shard_map/ppermute | solution.py:327
  (52 shorter events, 10.8 us)
Async XLA Ops:
  0.0 1.6 %collective-permute-start.1 = (bf16[512,128]{1,0:T(8,128)(2,1)}, bf16[512,128]{1,0:T(8,128)(2,1)S(1)}, u32[]{:S(2)}, u32[]{:S(2)}) collective-permute-start(bf16[512,128]{1,0:T(8,128)(2,1)} %param.10), channel_id=1, source_target_pairs={{0,8},{8,0},{1,9},{9,1},{2,10},{10,2},{3,11},{11,3},{4,12},{12,4},... | collective-permute-start | bytes 393224 | tf_op jit(solution)/shard_map/ppermute | solution.py:325
  0.0 1.7 %collective-permute-start.2 = (bf16[512,128]{1,0:T(8,128)(2,1)}, bf16[512,128]{1,0:T(8,128)(2,1)S(1)}, u32[]{:S(2)}, u32[]{:S(2)}) collective-permute-start(bf16[512,128]{1,0:T(8,128)(2,1)} %param.11), channel_id=1, source_target_pairs={{0,8},{8,0},{1,9},{9,1},{2,10},{10,2},{3,11},{11,3},{4,12},{12,4},... | collective-permute-start | bytes 393224 | tf_op jit(solution)/shard_map/ppermute | solution.py:325
  1.8 16.3 %collective-permute-start.3 = (bf16[1024,256]{1,0:T(8,128)(2,1)S(1)}, bf16[1024,256]{1,0:T(8,128)(2,1)S(1)}, u32[]{:S(2)}, u32[]{:S(2)}) collective-permute-start(bf16[1024,256]{1,0:T(8,128)(2,1)S(1)} %maximum_maximum_fusion.refs_1_.refs_4_), channel_id=1, source_target_pairs={{0,32},{8,232},{32,64},{40,8},{64,96},{72,40},{96,128},{104,72},{1... | collective-permute-start | bytes 1572872 | tf_op jit(solution)/shard_map/ppermute | solution.py:328
  3.8 18.9 %collective-permute-start.4 = (bf16[512,256]{1,0:T(8,128)(2,1)S(1)}, bf16[512,256]{1,0:T(8,128)(2,1)S(1)}, u32[]{:S(2)}, u32[]{:S(2)}) collective-permute-start(bf16[512,256]{1,0:T(8,128)(2,1)S(1)} %pad_maximum_fusion), channel_id=1, source_target_pairs={{0,16},{16,0},{1,17},{17,1},{2,18},{18,2},{3,19},{19,3},{4,20},{20... | collective-permute-start | bytes 786440 | tf_op jit(solution)/shard_map/ppermute | solution.py:326
  6.1 8.5 %collective-permute-start = (bf16[256,512]{1,0:T(8,128)(2,1)}, bf16[256,512]{1,0:T(8,128)(2,1)S(1)}, u32[]{:S(2)}, u32[]{:S(2)}) collective-permute-start(bf16[256,512]{1,0:T(8,128)(2,1)} %refs_0_.15), channel_id=1, source_target_pairs={{0,8},{8,0},{1,9},{9,1},{2,10},{10,2},{3,11},{11,3},{4,12},{12,4},... | collective-permute-start | bytes 786440 | tf_op jit(solution)/shard_map/ppermute | solution.py:325
  9.9 6.1 %copy-start = (s32[4]{0:T(128)S(1)}, s32[4]{0:T(128)}, u32[]{:S(2)}) copy-start(s32[4]{0:T(128)} %lengths.1) | copy-start | bytes 52
  9.9 6.1 %copy-start.1 = (bf16[256,512]{1,0:T(8,128)(2,1)S(1)}, bf16[256,512]{1,0:T(8,128)(2,1)}, u32[]{:S(2)}) copy-start(bf16[256,512]{1,0:T(8,128)(2,1)} %refs_0_.15) | copy-start | bytes 786436
  9.9 6.1 %copy-start.2 = (bf16[256,128]{1,0:T(8,128)(2,1)S(1)}, bf16[256,128]{1,0:T(8,128)(2,1)}, u32[]{:S(2)}) copy-start(bf16[256,128]{1,0:T(8,128)(2,1)} %refs_1_.1) | copy-start | bytes 196612
  9.9 6.1 %copy-start.3 = (bf16[256,128]{1,0:T(8,128)(2,1)S(1)}, bf16[256,128]{1,0:T(8,128)(2,1)}, u32[]{:S(2)}) copy-start(bf16[256,128]{1,0:T(8,128)(2,1)} %refs_2_.1) | copy-start | bytes 196612
  13.0 25.6 %collective-permute-start.8 = (bf16[512,1024]{1,0:T(8,128)(2,1)S(1)}, bf16[512,1024]{1,0:T(8,128)(2,1)S(1)}, u32[]{:S(2)}, u32[]{:S(2)}) collective-permute-start(bf16[512,1024]{1,0:T(8,128)(2,1)S(1)} %get-tuple-element.204), channel_id=1, source_target_pairs={{0,1},{1,2},{2,3},{3,0},{8,11},{9,8},{10,9},{11,10},{4,5},{5,6},{6... | collective-permute-start | bytes 3145736 | tf_op jit(solution)/shard_map/ppermute | solution.py:329
  18.1 17.3 %collective-permute-start.6 = (bf16[1024,256]{1,0:T(8,128)(2,1)S(1)}, bf16[1024,256]{1,0:T(8,128)(2,1)S(1)}, u32[]{:S(2)}, u32[]{:S(2)}) collective-permute-start(bf16[1024,256]{1,0:T(8,128)(2,1)S(1)} %collective-permute-done.3.refs_2_), channel_id=1, source_target_pairs={{0,16},{16,0},{1,17},{17,1},{2,18},{18,2},{3,19},{19,3},{4,20},{20... | collective-permute-start | bytes 1572872 | tf_op jit(solution)/shard_map/ppermute | solution.py:326
  19.4 10.4 %collective-permute-start.5 = (bf16[1024,256]{1,0:T(8,128)(2,1)S(1)}, bf16[1024,256]{1,0:T(8,128)(2,1)S(1)}, u32[]{:S(2)}, u32[]{:S(2)}) collective-permute-start(bf16[1024,256]{1,0:T(8,128)(2,1)S(1)} %collective-permute-done.3.refs_2_), channel_id=1, source_target_pairs={{0,32},{8,232},{32,64},{40,8},{64,96},{72,40},{96,128},{104,72},{1... | collective-permute-start | bytes 1572872 | tf_op jit(solution)/shard_map/ppermute | solution.py:328
  22.7 35.4 %collective-permute-start.13 = (bf16[1024,1024]{1,0:T(8,128)(2,1)S(1)}, bf16[1024,1024]{1,0:T(8,128)(2,1)S(1)}, u32[]{:S(2)}, u32[]{:S(2)}) collective-permute-start(bf16[1024,1024]{1,0:T(8,128)(2,1)S(1)} %get-tuple-element.239), channel_id=1, source_target_pairs={{0,1},{1,2},{2,3},{3,0},{8,11},{9,8},{10,9},{11,10},{4,5},{5,6},{6... | collective-permute-start | bytes 6291464 | tf_op jit(solution)/shard_map/ppermute | solution.py:329
  29.8 16.1 %collective-permute-start.9 = (bf16[1024,256]{1,0:T(8,128)(2,1)S(1)}, bf16[1024,256]{1,0:T(8,128)(2,1)S(1)}, u32[]{:S(2)}, u32[]{:S(2)}) collective-permute-start(bf16[1024,256]{1,0:T(8,128)(2,1)S(1)} %collective-permute-done.5.refs_2_), channel_id=1, source_target_pairs={{0,16},{16,0},{1,17},{17,1},{2,18},{18,2},{3,19},{19,3},{4,20},{20... | collective-permute-start | bytes 1572872 | tf_op jit(solution)/shard_map/ppermute | solution.py:326
  32.1 10.4 %collective-permute-start.7 = (bf16[1024,256]{1,0:T(8,128)(2,1)S(1)}, bf16[1024,256]{1,0:T(8,128)(2,1)S(1)}, u32[]{:S(2)}, u32[]{:S(2)}) collective-permute-start(bf16[1024,256]{1,0:T(8,128)(2,1)S(1)} %collective-permute-done.5.refs_2_), channel_id=1, source_target_pairs={{0,32},{8,232},{32,64},{40,8},{64,96},{72,40},{96,128},{104,72},{1... | collective-permute-start | bytes 1572872 | tf_op jit(solution)/shard_map/ppermute | solution.py:328
  42.5 7.7 %collective-permute-start.10 = (bf16[512,256]{1,0:T(8,128)(2,1)S(1)}, bf16[512,256]{1,0:T(8,128)(2,1)S(1)}, u32[]{:S(2)}, u32[]{:S(2)}) collective-permute-start(bf16[512,256]{1,0:T(8,128)(2,1)S(1)} %slice.3), channel_id=1, source_target_pairs={{0,32},{8,232},{32,64},{40,8},{64,96},{72,40},{96,128},{104,72},{1... | collective-permute-start | bytes 786440 | tf_op jit(solution)/shard_map/ppermute | solution.py:328
  45.9 12.2 %collective-permute-start.11 = (bf16[1024,256]{1,0:T(8,128)(2,1)S(1)}, bf16[1024,256]{1,0:T(8,128)(2,1)S(1)}, u32[]{:S(2)}, u32[]{:S(2)}) collective-permute-start(bf16[1024,256]{1,0:T(8,128)(2,1)S(1)} %collective-permute-done.9.refs_2_), channel_id=1, source_target_pairs={{0,32},{8,232},{32,64},{40,8},{64,96},{72,40},{96,128},{104,72},{1... | collective-permute-start | bytes 1572872 | tf_op jit(solution)/shard_map/ppermute | solution.py:328
  46.0 18.9 %collective-permute-start.16 = (bf16[512,1024]{1,0:T(8,128)(2,1)S(1)}, bf16[512,1024]{1,0:T(8,128)(2,1)S(1)}, u32[]{:S(2)}, u32[]{:S(2)}) collective-permute-start(bf16[512,1024]{1,0:T(8,128)(2,1)S(1)} %collective-permute-done.8), channel_id=1, source_target_pairs={{0,1},{1,2},{2,3},{3,0},{8,11},{9,8},{10,9},{11,10},{4,5},{5,6},{6... | collective-permute-start | bytes 3145736 | tf_op jit(solution)/shard_map/ppermute | solution.py:329
  50.2 7.9 %collective-permute-start.12 = (bf16[512,256]{1,0:T(8,128)(2,1)S(1)}, bf16[512,256]{1,0:T(8,128)(2,1)S(1)}, u32[]{:S(2)}, u32[]{:S(2)}) collective-permute-start(bf16[512,256]{1,0:T(8,128)(2,1)S(1)} %collective-permute-done.10.refs_3_), channel_id=1, source_target_pairs={{0,16},{16,0},{1,17},{17,1},{2,18},{18,2},{3,19},{19,3},{4,20},{20... | collective-permute-start | bytes 786440 | tf_op jit(solution)/shard_map/ppermute | solution.py:326
  58.1 21.1 %collective-permute-start.20 = (bf16[1024,1024]{1,0:T(8,128)(2,1)S(1)}, bf16[1024,1024]{1,0:T(8,128)(2,1)S(1)}, u32[]{:S(2)}, u32[]{:S(2)}) collective-permute-start(bf16[1024,1024]{1,0:T(8,128)(2,1)S(1)} %collective-permute-done.13.w_first), channel_id=1, source_target_pairs={{0,8},{8,0},{1,9},{9,1},{2,10},{10,2},{3,11},{11,3},{4,12},{12,4},... | collective-permute-start | bytes 6291464 | tf_op jit(solution)/shard_map/ppermute | solution.py:325
  60.6 3.3 %collective-permute-start.15 = (f32[256,128]{1,0:T(8,128)S(1)}, f32[256,128]{1,0:T(8,128)S(1)}, u32[]{:S(2)}, u32[]{:S(2)}) collective-permute-start(f32[256,128]{1,0:T(8,128)S(1)} %get-tuple-element.260), channel_id=1, source_target_pairs={{0,8},{8,0},{1,9},{9,1},{2,10},{10,2},{3,11},{11,3},{4,12},{12,4},... | collective-permute-start | bytes 393224 | tf_op jit(solution)/shard_map/ppermute | solution.py:325
  61.2 2.7 %collective-permute-start.14 = (bf16[256,512]{1,0:T(8,128)(2,1)S(1)}, bf16[256,512]{1,0:T(8,128)(2,1)S(1)}, u32[]{:S(2)}, u32[]{:S(2)}) collective-permute-start(bf16[256,512]{1,0:T(8,128)(2,1)S(1)} %get-tuple-element.259), channel_id=1, source_target_pairs={{0,8},{8,0},{1,9},{9,1},{2,10},{10,2},{3,11},{11,3},{4,12},{12,4},... | collective-permute-start | bytes 786440 | tf_op jit(solution)/shard_map/ppermute | solution.py:325
  64.9 14.3 %collective-permute-start.21 = (bf16[512,1024]{1,0:T(8,128)(2,1)S(1)}, bf16[512,1024]{1,0:T(8,128)(2,1)S(1)}, u32[]{:S(2)}, u32[]{:S(2)}) collective-permute-start(bf16[512,1024]{1,0:T(8,128)(2,1)S(1)} %collective-permute-done.16.w_mine), channel_id=1, source_target_pairs={{0,8},{8,0},{1,9},{9,1},{2,10},{10,2},{3,11},{11,3},{4,12},{12,4},... | collective-permute-start | bytes 3145736 | tf_op jit(solution)/shard_map/ppermute | solution.py:325
  65.2 6.8 %collective-permute-start.17 = (bf16[128,512]{1,0:T(8,128)(2,1)S(1)}, bf16[128,512]{1,0:T(8,128)(2,1)S(1)}, u32[]{:S(2)}, u32[]{:S(2)}) collective-permute-start(bf16[128,512]{1,0:T(8,128)(2,1)S(1)} %get-tuple-element.264.own), channel_id=1, source_target_pairs={{0,1},{1,2},{2,3},{3,0},{8,11},{9,8},{10,9},{11,10},{4,5},{5,6},{6... | collective-permute-start | bytes 393224 | tf_op jit(solution)/shard_map/ppermute | solution.py:329
  66.6 6.0 %collective-permute-start.18 = (bf16[128,512]{1,0:T(8,128)(2,1)S(1)}, bf16[128,512]{1,0:T(8,128)(2,1)S(1)}, u32[]{:S(2)}, u32[]{:S(2)}) collective-permute-start(bf16[128,512]{1,0:T(8,128)(2,1)S(1)} %get-tuple-element.264.own), channel_id=1, source_target_pairs={{0,3},{1,0},{2,1},{3,2},{8,9},{9,10},{10,11},{11,8},{4,7},{5,4},{6... | collective-permute-start | bytes 393224 | tf_op jit(solution)/shard_map/ppermute | solution.py:330
  68.4 7.1 %collective-permute-start.22 = (bf16[128,512]{1,0:T(8,128)(2,1)S(1)}, bf16[128,512]{1,0:T(8,128)(2,1)S(1)}, u32[]{:S(2)}, u32[]{:S(2)}) collective-permute-start(bf16[128,512]{1,0:T(8,128)(2,1)S(1)} %get-tuple-element.268.own), channel_id=1, source_target_pairs={{0,1},{1,2},{2,3},{3,0},{8,11},{9,8},{10,9},{11,10},{4,5},{5,6},{6... | collective-permute-start | bytes 393224 | tf_op jit(solution)/shard_map/ppermute | solution.py:329
  72.0 7.2 %collective-permute-start.19 = (bf16[128,512]{1,0:T(8,128)(2,1)S(1)}, bf16[128,512]{1,0:T(8,128)(2,1)S(1)}, u32[]{:S(2)}, u32[]{:S(2)}) collective-permute-start(bf16[128,512]{1,0:T(8,128)(2,1)S(1)} %collective-permute-done.17.first), channel_id=1, source_target_pairs={{0,1},{1,2},{2,3},{3,0},{8,11},{9,8},{10,9},{11,10},{4,5},{5,6},{6... | collective-permute-start | bytes 393224 | tf_op jit(solution)/shard_map/ppermute | solution.py:329
  72.6 8.7 %collective-permute-start.23 = (bf16[128,512]{1,0:T(8,128)(2,1)S(1)}, bf16[128,512]{1,0:T(8,128)(2,1)S(1)}, u32[]{:S(2)}, u32[]{:S(2)}) collective-permute-start(bf16[128,512]{1,0:T(8,128)(2,1)S(1)} %get-tuple-element.268.own), channel_id=1, source_target_pairs={{0,3},{1,0},{2,1},{3,2},{8,9},{9,10},{10,11},{11,8},{4,7},{5,4},{6... | collective-permute-start | bytes 393224 | tf_op jit(solution)/shard_map/ppermute | solution.py:330
  75.5 6.2 %collective-permute-start.24 = (bf16[128,512]{1,0:T(8,128)(2,1)S(1)}, bf16[128,512]{1,0:T(8,128)(2,1)S(1)}, u32[]{:S(2)}, u32[]{:S(2)}) collective-permute-start(bf16[128,512]{1,0:T(8,128)(2,1)S(1)} %collective-permute-done.22.first), channel_id=1, source_target_pairs={{0,1},{1,2},{2,3},{3,0},{8,11},{9,8},{10,9},{11,10},{4,5},{5,6},{6... | collective-permute-start | bytes 393224 | tf_op jit(solution)/shard_map/ppermute | solution.py:329
  79.9 8.1 %collective-permute-start.25 = (bf16[128,1024]{1,0:T(8,128)(2,1)S(1)}, bf16[128,1024]{1,0:T(8,128)(2,1)S(1)}, u32[]{:S(2)}, u32[]{:S(2)}) collective-permute-start(bf16[128,1024]{1,0:T(8,128)(2,1)S(1)} %project.6), channel_id=1, source_target_pairs={{0,4},{4,0},{1,5},{5,1},{2,6},{6,2},{3,7},{7,3},{8,12},{12,8},{9,1... | collective-permute-start | bytes 786440 | tf_op jit(solution)/shard_map/ppermute | solution.py:327
  82.4 8.4 %collective-permute-start.26 = (bf16[128,1024]{1,0:T(8,128)(2,1)S(1)}, bf16[128,1024]{1,0:T(8,128)(2,1)S(1)}, u32[]{:S(2)}, u32[]{:S(2)}) collective-permute-start(bf16[128,1024]{1,0:T(8,128)(2,1)S(1)} %project.7), channel_id=1, source_target_pairs={{0,4},{4,0},{1,5},{5,1},{2,6},{6,2},{3,7},{7,3},{8,12},{12,8},{9,1... | collective-permute-start | bytes 786440 | tf_op jit(solution)/shard_map/ppermute | solution.py:327

commit v3 on v2

--- a/solution.py
+++ b/solution.py
@@ -105,7 +105,7 @@
     old = None if first else [[refs.pop(0) for _ in range(3)] for _ in range(sets)]
     new = [[refs.pop(0) for _ in range(3)] for _ in range(sets)]
     slots = queries[0].shape[0]
-    turns = 2
+    turns = 1 if first and not with_self else 2
 
     def at(tile):
         return pl.ds(pl.multiple_of(tile[1] * slots, slots), slots)

time: 91.9 us -> 91.5 us (level)
  transfers between devices with their start and end apart: 27 -> 27, of which waited for: 10 -> 10; matrix products, arithmetic and copies ran while one was open for 1% -> 1% of each run, Pallas kernels for 38% -> 37%
where the time goes in v3:
time: 91.5 us
  Pallas kernels  34.2 us (37%)
  starting transfers between devices  29.3 us (32%)
  waiting for transfers between devices  25.5 us (28%)
  other arithmetic  2.03 us (2%)
    pallas_call x10, Pallas kernels, attend(): pl.pallas_call(functools.partial(attend_kernel, scale, group, resp_len, s...  27.1 us
    ppermute x5, waiting for transfers between devices, per_device(): z_hop = lambda v: lax.ppermute(v, ('z', 'core'), opposite(z_size, 1))  10.2 us
    ppermute x7, waiting for transfers between devices, per_device(): x_near = lambda v: lax.ppermute(v, ('core', 'x'), opposite_x(x_size, 1))  7.32 us
    ppermute x4, starting transfers between devices, per_device(): swap_yh = lambda v: lax.ppermute(v, 'yh', ring(2, 1))  7.14 us
    ppermute x7, starting transfers between devices, per_device(): x_near = lambda v: lax.ppermute(v, ('core', 'x'), opposite_x(x_size, 1))  7.1 us
    ppermute x2, waiting for transfers between devices, per_device(): swap_yl = lambda v: lax.ppermute(v, 'yl', ring(2, 1))  5.52 us
    ppermute x7, starting transfers between devices, per_device(): swap_core = lambda v: lax.ppermute(v, 'core', ring(2, 1))  5.4 us
    ppermute x2, starting transfers between devices, per_device(): x_back = lambda v: lax.ppermute(v, ('core', 'x'), opposite_x(x_size, -1))  4.65 us
  transfers between devices with their start and end apart: 27, of which 10 were waited for; matrix products, arithmetic and copies ran while one was open for 1% of the time, Pallas kernels for 37%

profile of v3, /device:TPU:8, one launch (start us, length us, event | category | flops | bytes accessed | tf_op | source)
XLA Modules:
  0.0 91.5 jit_solution(16605762570684828175)
XLA Ops:
  1.8 2.0 %collective-permute-start.3 = (bf16[1024,256]{1,0:T(8,128)(2,1)S(1)}, bf16[1024,256]{1,0:T(8,128)(2,1)S(1)}, u32[]{:S(2)}, u32[]{:S(2)}) collective-permute-start(bf16[1024,256]{1,0:T(8,128)(2,1)S(1)} %maximum_maximum_fusion.refs_1_.refs_4_), channel_id=1, source_target_pairs={{0,32},{8,232},{32,64},{40,8},{64,96},{72,40},{96,128},{104,72},{1... | collective-permute-start | bytes 1572872 | tf_op jit(solution)/shard_map/ppermute | solution.py:328
  3.8 2.3 %collective-permute-start.4 = (bf16[512,256]{1,0:T(8,128)(2,1)S(1)}, bf16[512,256]{1,0:T(8,128)(2,1)S(1)}, u32[]{:S(2)}, u32[]{:S(2)}) collective-permute-start(bf16[512,256]{1,0:T(8,128)(2,1)S(1)} %pad_maximum_fusion), channel_id=1, source_target_pairs={{0,16},{16,0},{1,17},{17,1},{2,18},{18,2},{3,19},{19,3},{4,20},{20... | collective-permute-start | bytes 786440 | tf_op jit(solution)/shard_map/ppermute | solution.py:326
  6.1 3.7 %collective-permute-start = (bf16[256,512]{1,0:T(8,128)(2,1)}, bf16[256,512]{1,0:T(8,128)(2,1)S(1)}, u32[]{:S(2)}, u32[]{:S(2)}) collective-permute-start(bf16[256,512]{1,0:T(8,128)(2,1)} %refs_0_.15), channel_id=1, source_target_pairs={{0,8},{8,0},{1,9},{9,1},{2,10},{10,2},{3,11},{11,3},{4,12},{12,4},... | collective-permute-start | bytes 786440 | tf_op jit(solution)/shard_map/ppermute | solution.py:325
  9.9 3.1 %cut.1 = (bf16[1024,1024]{1,0:T(8,128)(2,1)S(1)}, bf16[512,1024]{1,0:T(8,128)(2,1)S(1)}, bf16[1024,1024]{1,0:T(8,128)(2,1)S(1)}) custom-call(s32[7]{0:T(128)S(1)} %stack.31.places, bf16[512,8192]{1,0:T(8,128)(2,1)} %weight.1), custom_call_target="tpu_custom_call" | custom-call | flops 4294967296 | bytes 1048576 | tf_op jit(solution)/shard_map/cut/pallas_call | solution.py:273
  13.0 1.6 %collective-permute-start.8 = (bf16[512,1024]{1,0:T(8,128)(2,1)S(1)}, bf16[512,1024]{1,0:T(8,128)(2,1)S(1)}, u32[]{:S(2)}, u32[]{:S(2)}) collective-permute-start(bf16[512,1024]{1,0:T(8,128)(2,1)S(1)} %get-tuple-element.204), channel_id=1, source_target_pairs={{0,1},{1,2},{2,3},{3,0},{8,11},{9,8},{10,9},{11,10},{4,5},{5,6},{6... | collective-permute-start | bytes 3145736 | tf_op jit(solution)/shard_map/ppermute | solution.py:329
  15.6 2.1 %attend.11 = (f32[1024,128]{1,0:T(8,128)S(1)}, f32[1024,128]{1,0:T(8,128)S(1)}, f32[1024,128]{1,0:T(8,128)S(1)}) custom-call(s32[4]{0:T(128)S(1)} %copy-done, bf16[256,128]{1,0:T(8,128)(2,1)S(1)} %copy-done.2, bf16[256,128]{1,0:T(8,128)(2,1)S(1)} %copy-done.3, bf16[256,512]{1,0:T(8,128)(2,1)S(1)} %copy-done.1, ...), custom_call_target="tpu_custom_call" | custom-call | flops 536870912 | bytes 65536 | tf_op jit(solution)/shard_map/attend/pallas_call | solution.py:172
  17.7 1.3 %collective-permute-start.6 = (bf16[1024,256]{1,0:T(8,128)(2,1)S(1)}, bf16[1024,256]{1,0:T(8,128)(2,1)S(1)}, u32[]{:S(2)}, u32[]{:S(2)}) collective-permute-start(bf16[1024,256]{1,0:T(8,128)(2,1)S(1)} %collective-permute-done.3.refs_2_), channel_id=1, source_target_pairs={{0,16},{16,0},{1,17},{17,1},{2,18},{18,2},{3,19},{19,3},{4,20},{20... | collective-permute-start | bytes 1572872 | tf_op jit(solution)/shard_map/ppermute | solution.py:326
  19.0 3.2 %attend.12 = (f32[1024,128]{1,0:T(8,128)S(1)}, f32[1024,128]{1,0:T(8,128)S(1)}, f32[1024,128]{1,0:T(8,128)S(1)}, f32[1024,128]{1,0:T(8,128)S(1)}, f32[1024,128]{1,0:T(8,128)S(1)}, /*index=5*/f32[1024,128]{1,0:T(8,128)S(1)}) custom-call(bf16[256,512]{1,0:T(8,128)(2,1)S(1)} %copy-done.1, ...), custom_call_target="tpu_custom_call", output_to_operand_aliasing={{0}: (3, {}), {1}: (4, {}), {2}: (5, {}), {3}: (6, {}), {4}... | custom-call | flops 8589934592 | bytes 65536 | tf_op jit(solution)/shard_map/attend/pallas_call | solution.py:172
  22.3 1.6 %collective-permute-start.13 = (bf16[1024,1024]{1,0:T(8,128)(2,1)S(1)}, bf16[1024,1024]{1,0:T(8,128)(2,1)S(1)}, u32[]{:S(2)}, u32[]{:S(2)}) collective-permute-start(bf16[1024,1024]{1,0:T(8,128)(2,1)S(1)} %get-tuple-element.239), channel_id=1, source_target_pairs={{0,1},{1,2},{2,3},{3,0},{8,11},{9,8},{10,9},{11,10},{4,5},{5,6},{6... | collective-permute-start | bytes 6291464 | tf_op jit(solution)/shard_map/ppermute | solution.py:329
  23.9 1.9 %attend.13 = (f32[1024,128]{1,0:T(8,128)S(1)}, f32[1024,128]{1,0:T(8,128)S(1)}, f32[1024,128]{1,0:T(8,128)S(1)}, f32[1024,128]{1,0:T(8,128)S(1)}, f32[1024,128]{1,0:T(8,128)S(1)}, /*index=5*/f32[1024,128]{1,0:T(8,128)S(1)}) custom-call(bf16[256,512]{1,0:T(8,128)(2,1)S(1)} %copy-done.1, ...), custom_call_target="tpu_custom_call", output_to_operand_aliasing={{0}: (3, {}), {1}: (4, {}), {2}: (5, {}), {3}: (6, {}), {4}... | custom-call | flops 4294967296 | bytes 65536 | tf_op jit(solution)/shard_map/attend/pallas_call | solution.py:172
  25.8 3.6 %collective-permute-done.5.refs_2_ = bf16[1024,256]{1,0:T(8,128)(2,1)S(1)} collective-permute-done((bf16[1024,256]{1,0:T(8,128)(2,1)S(1)}, bf16[1024,256]{1,0:T(8,128)(2,1)S(1)}, u32[]{:S(2)}, u32[]{:S(2)}) %collective-permute-start.5) | collective-permute-done | bytes 524320 | tf_op jit(solution)/shard_map/ppermute | solution.py:328
  29.4 2.3 %collective-permute-start.9 = (bf16[1024,256]{1,0:T(8,128)(2,1)S(1)}, bf16[1024,256]{1,0:T(8,128)(2,1)S(1)}, u32[]{:S(2)}, u32[]{:S(2)}) collective-permute-start(bf16[1024,256]{1,0:T(8,128)(2,1)S(1)} %collective-permute-done.5.refs_2_), channel_id=1, source_target_pairs={{0,16},{16,0},{1,17},{17,1},{2,18},{18,2},{3,19},{19,3},{4,20},{20... | collective-permute-start | bytes 1572872 | tf_op jit(solution)/shard_map/ppermute | solution.py:326
  31.7 3.2 %attend.14 = (f32[1024,128]{1,0:T(8,128)S(1)}, f32[1024,128]{1,0:T(8,128)S(1)}, f32[1024,128]{1,0:T(8,128)S(1)}, f32[1024,128]{1,0:T(8,128)S(1)}, f32[1024,128]{1,0:T(8,128)S(1)}, /*index=5*/f32[1024,128]{1,0:T(8,128)S(1)}) custom-call(bf16[256,512]{1,0:T(8,128)(2,1)S(1)} %copy-done.1, ...), custom_call_target="tpu_custom_call", output_to_operand_aliasing={{0}: (3, {}), {1}: (4, {}), {2}: (5, {}), {3}: (6, {}), {4}... | custom-call | flops 4294967296 | bytes 65536 | tf_op jit(solution)/shard_map/attend/pallas_call | solution.py:172
  35.0 3.2 %attend.15 = (f32[1024,128]{1,0:T(8,128)S(1)}, f32[1024,128]{1,0:T(8,128)S(1)}, f32[1024,128]{1,0:T(8,128)S(1)}, f32[1024,128]{1,0:T(8,128)S(1)}, f32[1024,128]{1,0:T(8,128)S(1)}, /*index=5*/f32[1024,128]{1,0:T(8,128)S(1)}) custom-call(bf16[256,512]{1,0:T(8,128)(2,1)S(1)} %copy-done.1, ...), custom_call_target="tpu_custom_call", output_to_operand_aliasing={{0}: (3, {}), {1}: (4, {}), {2}: (5, {}), {3}: (6, {}), {4}... | custom-call | flops 4294967296 | bytes 65536 | tf_op jit(solution)/shard_map/attend/pallas_call | solution.py:172
  38.2 3.9 %collective-permute-done.7.refs_2_ = bf16[1024,256]{1,0:T(8,128)(2,1)S(1)} collective-permute-done((bf16[1024,256]{1,0:T(8,128)(2,1)S(1)}, bf16[1024,256]{1,0:T(8,128)(2,1)S(1)}, u32[]{:S(2)}, u32[]{:S(2)}) %collective-permute-start.7) | collective-permute-done | bytes 524320 | tf_op jit(solution)/shard_map/ppermute | solution.py:328
  42.2 3.2 %attend.16 = (f32[1024,128]{1,0:T(8,128)S(1)}, f32[1024,128]{1,0:T(8,128)S(1)}, f32[1024,128]{1,0:T(8,128)S(1)}, f32[1024,128]{1,0:T(8,128)S(1)}, f32[1024,128]{1,0:T(8,128)S(1)}, /*index=5*/f32[1024,128]{1,0:T(8,128)S(1)}) custom-call(bf16[256,512]{1,0:T(8,128)(2,1)S(1)} %copy-done.1, ...), custom_call_target="tpu_custom_call", output_to_operand_aliasing={{0}: (3, {}), {1}: (4, {}), {2}: (5, {}), {3}: (6, {}), {4}... | custom-call | flops 4294967296 | bytes 65536 | tf_op jit(solution)/shard_map/attend/pallas_call | solution.py:172
  45.6 1.6 %collective-permute-start.16 = (bf16[512,1024]{1,0:T(8,128)(2,1)S(1)}, bf16[512,1024]{1,0:T(8,128)(2,1)S(1)}, u32[]{:S(2)}, u32[]{:S(2)}) collective-permute-start(bf16[512,1024]{1,0:T(8,128)(2,1)S(1)} %collective-permute-done.8), channel_id=1, source_target_pairs={{0,1},{1,2},{2,3},{3,0},{8,11},{9,8},{10,9},{11,10},{4,5},{5,6},{6... | collective-permute-start | bytes 3145736 | tf_op jit(solution)/shard_map/ppermute | solution.py:329
  47.1 2.7 %collective-permute-done.10.refs_3_ = bf16[512,256]{1,0:T(8,128)(2,1)S(1)} collective-permute-done((bf16[512,256]{1,0:T(8,128)(2,1)S(1)}, bf16[512,256]{1,0:T(8,128)(2,1)S(1)}, u32[]{:S(2)}, u32[]{:S(2)}) %collective-permute-start.10) | collective-permute-done | bytes 262176 | tf_op jit(solution)/shard_map/ppermute | solution.py:328
  49.8 1.2 %collective-permute-start.12 = (bf16[512,256]{1,0:T(8,128)(2,1)S(1)}, bf16[512,256]{1,0:T(8,128)(2,1)S(1)}, u32[]{:S(2)}, u32[]{:S(2)}) collective-permute-start(bf16[512,256]{1,0:T(8,128)(2,1)S(1)} %collective-permute-done.10.refs_3_), channel_id=1, source_target_pairs={{0,16},{16,0},{1,17},{17,1},{2,18},{18,2},{3,19},{19,3},{4,20},{20... | collective-permute-start | bytes 786440 | tf_op jit(solution)/shard_map/ppermute | solution.py:326
  51.0 4.4 %attend.17 = (f32[1024,128]{1,0:T(8,128)S(1)}, f32[1024,128]{1,0:T(8,128)S(1)}, f32[1024,128]{1,0:T(8,128)S(1)}, f32[1024,128]{1,0:T(8,128)S(1)}, f32[1024,128]{1,0:T(8,128)S(1)}, /*index=5*/f32[1024,128]{1,0:T(8,128)S(1)}) custom-call(bf16[256,512]{1,0:T(8,128)(2,1)S(1)} %copy-done.1, ...), custom_call_target="tpu_custom_call", output_to_operand_aliasing={{0}: (4, {}), {1}: (5, {}), {2}: (6, {}), {3}: (7, {}), {4}... | custom-call | flops 6442450944 | bytes 65536 | tf_op jit(solution)/shard_map/attend/pallas_call | solution.py:172
  55.4 2.2 %collective-permute-done.12.refs_2_ = bf16[512,256]{1,0:T(8,128)(2,1)S(1)} collective-permute-done((bf16[512,256]{1,0:T(8,128)(2,1)S(1)}, bf16[512,256]{1,0:T(8,128)(2,1)S(1)}, u32[]{:S(2)}, u32[]{:S(2)}) %collective-permute-start.12) | collective-permute-done | bytes 262176 | tf_op jit(solution)/shard_map/ppermute | solution.py:326
  57.7 2.4 %attend.18 = (f32[1024,128]{1,0:T(8,128)S(1)}, f32[1024,128]{1,0:T(8,128)S(1)}, f32[1024,128]{1,0:T(8,128)S(1)}) custom-call(bf16[256,512]{1,0:T(8,128)(2,1)S(1)} %collective-permute-done.refs_0_.refs_1_, bf16[1024,256]{1,0:T(8,128)(2,1)S(1)} %collective-permute-done.11.refs_1_, ...), custom_call_target="tpu_custom_call", output_to_operand_aliasing={{0}: (3, {}), {1}: (4, {}), {2}: (5, {})} | custom-call | flops 3221225472 | bytes 65536 | tf_op jit(solution)/shard_map/attend/pallas_call | solution.py:172
  61.1 2.4 %attend.19 = (f32[1024,128]{1,0:T(8,128)S(1)}, f32[1024,128]{1,0:T(8,128)S(1)}, f32[1024,128]{1,0:T(8,128)S(1)}) custom-call(bf16[256,512]{1,0:T(8,128)(2,1)S(1)} %copy-done.1, bf16[1024,256]{1,0:T(8,128)(2,1)S(1)} %collective-permute-done.11.refs_1_, ...), custom_call_target="tpu_custom_call", output_to_operand_aliasing={{0}: (3, {}), {1}: (4, {}), {2}: (5, {})} | custom-call | flops 3221225472 | bytes 65536 | tf_op jit(solution)/shard_map/attend/pallas_call | solution.py:172
  64.8 1.5 %collective-permute-start.17 = (bf16[128,512]{1,0:T(8,128)(2,1)S(1)}, bf16[128,512]{1,0:T(8,128)(2,1)S(1)}, u32[]{:S(2)}, u32[]{:S(2)}) collective-permute-start(bf16[128,512]{1,0:T(8,128)(2,1)S(1)} %get-tuple-element.264.own), channel_id=1, source_target_pairs={{0,1},{1,2},{2,3},{3,0},{8,11},{9,8},{10,9},{11,10},{4,5},{5,6},{6... | collective-permute-start | bytes 393224 | tf_op jit(solution)/shard_map/ppermute | solution.py:329
  66.3 1.8 %collective-permute-start.18 = (bf16[128,512]{1,0:T(8,128)(2,1)S(1)}, bf16[128,512]{1,0:T(8,128)(2,1)S(1)}, u32[]{:S(2)}, u32[]{:S(2)}) collective-permute-start(bf16[128,512]{1,0:T(8,128)(2,1)S(1)} %get-tuple-element.264.own), channel_id=1, source_target_pairs={{0,3},{1,0},{2,1},{3,2},{8,9},{9,10},{10,11},{11,8},{4,7},{5,4},{6... | collective-permute-start | bytes 393224 | tf_op jit(solution)/shard_map/ppermute | solution.py:330
  68.3 3.3 %collective-permute-done.17.first = bf16[128,512]{1,0:T(8,128)(2,1)S(1)} collective-permute-done((bf16[128,512]{1,0:T(8,128)(2,1)S(1)}, bf16[128,512]{1,0:T(8,128)(2,1)S(1)}, u32[]{:S(2)}, u32[]{:S(2)}) %collective-permute-start.17) | collective-permute-done | bytes 131104 | tf_op jit(solution)/shard_map/ppermute | solution.py:329
  72.3 2.9 %collective-permute-start.23 = (bf16[128,512]{1,0:T(8,128)(2,1)S(1)}, bf16[128,512]{1,0:T(8,128)(2,1)S(1)}, u32[]{:S(2)}, u32[]{:S(2)}) collective-permute-start(bf16[128,512]{1,0:T(8,128)(2,1)S(1)} %get-tuple-element.268.own), channel_id=1, source_target_pairs={{0,3},{1,0},{2,1},{3,2},{8,9},{9,10},{10,11},{11,8},{4,7},{5,4},{6... | collective-permute-start | bytes 393224 | tf_op jit(solution)/shard_map/ppermute | solution.py:330
  75.2 3.6 %collective-permute-done.19.far = bf16[128,512]{1,0:T(8,128)(2,1)S(1)} collective-permute-done((bf16[128,512]{1,0:T(8,128)(2,1)S(1)}, bf16[128,512]{1,0:T(8,128)(2,1)S(1)}, u32[]{:S(2)}, u32[]{:S(2)}) %collective-permute-start.19) | collective-permute-done | bytes 131104 | tf_op jit(solution)/shard_map/ppermute | solution.py:329
  79.5 1.4 %collective-permute-start.25 = (bf16[128,1024]{1,0:T(8,128)(2,1)S(1)}, bf16[128,1024]{1,0:T(8,128)(2,1)S(1)}, u32[]{:S(2)}, u32[]{:S(2)}) collective-permute-start(bf16[128,1024]{1,0:T(8,128)(2,1)S(1)} %project.6), channel_id=1, source_target_pairs={{0,4},{4,0},{1,5},{5,1},{2,6},{6,2},{3,7},{7,3},{8,12},{12,8},{9,1... | collective-permute-start | bytes 786440 | tf_op jit(solution)/shard_map/ppermute | solution.py:327
  82.1 1.4 %collective-permute-start.26 = (bf16[128,1024]{1,0:T(8,128)(2,1)S(1)}, bf16[128,1024]{1,0:T(8,128)(2,1)S(1)}, u32[]{:S(2)}, u32[]{:S(2)}) collective-permute-start(bf16[128,1024]{1,0:T(8,128)(2,1)S(1)} %project.7), channel_id=1, source_target_pairs={{0,4},{4,0},{1,5},{5,1},{2,6},{6,2},{3,7},{7,3},{8,12},{12,8},{9,1... | collective-permute-start | bytes 786440 | tf_op jit(solution)/shard_map/ppermute | solution.py:327
  84.9 2.7 %collective-permute-done.25 = bf16[128,1024]{1,0:T(8,128)(2,1)S(1)} collective-permute-done((bf16[128,1024]{1,0:T(8,128)(2,1)S(1)}, bf16[128,1024]{1,0:T(8,128)(2,1)S(1)}, u32[]{:S(2)}, u32[]{:S(2)}) %collective-permute-start.25) | collective-permute-done | bytes 262176 | tf_op jit(solution)/shard_map/ppermute | solution.py:327
  87.7 2.8 %collective-permute-done.26 = bf16[128,1024]{1,0:T(8,128)(2,1)S(1)} collective-permute-done((bf16[128,1024]{1,0:T(8,128)(2,1)S(1)}, bf16[128,1024]{1,0:T(8,128)(2,1)S(1)}, u32[]{:S(2)}, u32[]{:S(2)}) %collective-permute-start.26) | collective-permute-done | bytes 262176 | tf_op jit(solution)/shard_map/ppermute | solution.py:327
  (52 shorter events, 10.5 us)
Async XLA Ops:
  0.0 1.6 %collective-permute-start.1 = (bf16[512,128]{1,0:T(8,128)(2,1)}, bf16[512,128]{1,0:T(8,128)(2,1)S(1)}, u32[]{:S(2)}, u32[]{:S(2)}) collective-permute-start(bf16[512,128]{1,0:T(8,128)(2,1)} %param.10), channel_id=1, source_target_pairs={{0,8},{8,0},{1,9},{9,1},{2,10},{10,2},{3,11},{11,3},{4,12},{12,4},... | collective-permute-start | bytes 393224 | tf_op jit(solution)/shard_map/ppermute | solution.py:325
  0.0 1.7 %collective-permute-start.2 = (bf16[512,128]{1,0:T(8,128)(2,1)}, bf16[512,128]{1,0:T(8,128)(2,1)S(1)}, u32[]{:S(2)}, u32[]{:S(2)}) collective-permute-start(bf16[512,128]{1,0:T(8,128)(2,1)} %param.11), channel_id=1, source_target_pairs={{0,8},{8,0},{1,9},{9,1},{2,10},{10,2},{3,11},{11,3},{4,12},{12,4},... | collective-permute-start | bytes 393224 | tf_op jit(solution)/shard_map/ppermute | solution.py:325
  1.8 15.9 %collective-permute-start.3 = (bf16[1024,256]{1,0:T(8,128)(2,1)S(1)}, bf16[1024,256]{1,0:T(8,128)(2,1)S(1)}, u32[]{:S(2)}, u32[]{:S(2)}) collective-permute-start(bf16[1024,256]{1,0:T(8,128)(2,1)S(1)} %maximum_maximum_fusion.refs_1_.refs_4_), channel_id=1, source_target_pairs={{0,32},{8,232},{32,64},{40,8},{64,96},{72,40},{96,128},{104,72},{1... | collective-permute-start | bytes 1572872 | tf_op jit(solution)/shard_map/ppermute | solution.py:328
  3.8 18.5 %collective-permute-start.4 = (bf16[512,256]{1,0:T(8,128)(2,1)S(1)}, bf16[512,256]{1,0:T(8,128)(2,1)S(1)}, u32[]{:S(2)}, u32[]{:S(2)}) collective-permute-start(bf16[512,256]{1,0:T(8,128)(2,1)S(1)} %pad_maximum_fusion), channel_id=1, source_target_pairs={{0,16},{16,0},{1,17},{17,1},{2,18},{18,2},{3,19},{19,3},{4,20},{20... | collective-permute-start | bytes 786440 | tf_op jit(solution)/shard_map/ppermute | solution.py:326
  6.1 8.5 %collective-permute-start = (bf16[256,512]{1,0:T(8,128)(2,1)}, bf16[256,512]{1,0:T(8,128)(2,1)S(1)}, u32[]{:S(2)}, u32[]{:S(2)}) collective-permute-start(bf16[256,512]{1,0:T(8,128)(2,1)} %refs_0_.15), channel_id=1, source_target_pairs={{0,8},{8,0},{1,9},{9,1},{2,10},{10,2},{3,11},{11,3},{4,12},{12,4},... | collective-permute-start | bytes 786440 | tf_op jit(solution)/shard_map/ppermute | solution.py:325
  9.9 5.7 %copy-start = (s32[4]{0:T(128)S(1)}, s32[4]{0:T(128)}, u32[]{:S(2)}) copy-start(s32[4]{0:T(128)} %lengths.1) | copy-start | bytes 52
  9.9 5.7 %copy-start.1 = (bf16[256,512]{1,0:T(8,128)(2,1)S(1)}, bf16[256,512]{1,0:T(8,128)(2,1)}, u32[]{:S(2)}) copy-start(bf16[256,512]{1,0:T(8,128)(2,1)} %refs_0_.15) | copy-start | bytes 786436
  9.9 5.7 %copy-start.2 = (bf16[256,128]{1,0:T(8,128)(2,1)S(1)}, bf16[256,128]{1,0:T(8,128)(2,1)}, u32[]{:S(2)}) copy-start(bf16[256,128]{1,0:T(8,128)(2,1)} %refs_1_.1) | copy-start | bytes 196612
  9.9 5.7 %copy-start.3 = (bf16[256,128]{1,0:T(8,128)(2,1)S(1)}, bf16[256,128]{1,0:T(8,128)(2,1)}, u32[]{:S(2)}) copy-start(bf16[256,128]{1,0:T(8,128)(2,1)} %refs_2_.1) | copy-start | bytes 196612
  13.0 25.2 %collective-permute-start.8 = (bf16[512,1024]{1,0:T(8,128)(2,1)S(1)}, bf16[512,1024]{1,0:T(8,128)(2,1)S(1)}, u32[]{:S(2)}, u32[]{:S(2)}) collective-permute-start(bf16[512,1024]{1,0:T(8,128)(2,1)S(1)} %get-tuple-element.204), channel_id=1, source_target_pairs={{0,1},{1,2},{2,3},{3,0},{8,11},{9,8},{10,9},{11,10},{4,5},{5,6},{6... | collective-permute-start | bytes 3145736 | tf_op jit(solution)/shard_map/ppermute | solution.py:329
  17.7 17.3 %collective-permute-start.6 = (bf16[1024,256]{1,0:T(8,128)(2,1)S(1)}, bf16[1024,256]{1,0:T(8,128)(2,1)S(1)}, u32[]{:S(2)}, u32[]{:S(2)}) collective-permute-start(bf16[1024,256]{1,0:T(8,128)(2,1)S(1)} %collective-permute-done.3.refs_2_), channel_id=1, source_target_pairs={{0,16},{16,0},{1,17},{17,1},{2,18},{18,2},{3,19},{19,3},{4,20},{20... | collective-permute-start | bytes 1572872 | tf_op jit(solution)/shard_map/ppermute | solution.py:326
  19.0 10.4 %collective-permute-start.5 = (bf16[1024,256]{1,0:T(8,128)(2,1)S(1)}, bf16[1024,256]{1,0:T(8,128)(2,1)S(1)}, u32[]{:S(2)}, u32[]{:S(2)}) collective-permute-start(bf16[1024,256]{1,0:T(8,128)(2,1)S(1)} %collective-permute-done.3.refs_2_), channel_id=1, source_target_pairs={{0,32},{8,232},{32,64},{40,8},{64,96},{72,40},{96,128},{104,72},{1... | collective-permute-start | bytes 1572872 | tf_op jit(solution)/shard_map/ppermute | solution.py:328
  22.3 35.4 %collective-permute-start.13 = (bf16[1024,1024]{1,0:T(8,128)(2,1)S(1)}, bf16[1024,1024]{1,0:T(8,128)(2,1)S(1)}, u32[]{:S(2)}, u32[]{:S(2)}) collective-permute-start(bf16[1024,1024]{1,0:T(8,128)(2,1)S(1)} %get-tuple-element.239), channel_id=1, source_target_pairs={{0,1},{1,2},{2,3},{3,0},{8,11},{9,8},{10,9},{11,10},{4,5},{5,6},{6... | collective-permute-start | bytes 6291464 | tf_op jit(solution)/shard_map/ppermute | solution.py:329
  29.4 16.1 %collective-permute-start.9 = (bf16[1024,256]{1,0:T(8,128)(2,1)S(1)}, bf16[1024,256]{1,0:T(8,128)(2,1)S(1)}, u32[]{:S(2)}, u32[]{:S(2)}) collective-permute-start(bf16[1024,256]{1,0:T(8,128)(2,1)S(1)} %collective-permute-done.5.refs_2_), channel_id=1, source_target_pairs={{0,16},{16,0},{1,17},{17,1},{2,18},{18,2},{3,19},{19,3},{4,20},{20... | collective-permute-start | bytes 1572872 | tf_op jit(solution)/shard_map/ppermute | solution.py:326
  31.7 10.4 %collective-permute-start.7 = (bf16[1024,256]{1,0:T(8,128)(2,1)S(1)}, bf16[1024,256]{1,0:T(8,128)(2,1)S(1)}, u32[]{:S(2)}, u32[]{:S(2)}) collective-permute-start(bf16[1024,256]{1,0:T(8,128)(2,1)S(1)} %collective-permute-done.5.refs_2_), channel_id=1, source_target_pairs={{0,32},{8,232},{32,64},{40,8},{64,96},{72,40},{96,128},{104,72},{1... | collective-permute-start | bytes 1572872 | tf_op jit(solution)/shard_map/ppermute | solution.py:328
  42.1 7.7 %collective-permute-start.10 = (bf16[512,256]{1,0:T(8,128)(2,1)S(1)}, bf16[512,256]{1,0:T(8,128)(2,1)S(1)}, u32[]{:S(2)}, u32[]{:S(2)}) collective-permute-start(bf16[512,256]{1,0:T(8,128)(2,1)S(1)} %slice.3), channel_id=1, source_target_pairs={{0,32},{8,232},{32,64},{40,8},{64,96},{72,40},{96,128},{104,72},{1... | collective-permute-start | bytes 786440 | tf_op jit(solution)/shard_map/ppermute | solution.py:328
  45.5 12.2 %collective-permute-start.11 = (bf16[1024,256]{1,0:T(8,128)(2,1)S(1)}, bf16[1024,256]{1,0:T(8,128)(2,1)S(1)}, u32[]{:S(2)}, u32[]{:S(2)}) collective-permute-start(bf16[1024,256]{1,0:T(8,128)(2,1)S(1)} %collective-permute-done.9.refs_2_), channel_id=1, source_target_pairs={{0,32},{8,232},{32,64},{40,8},{64,96},{72,40},{96,128},{104,72},{1... | collective-permute-start | bytes 1572872 | tf_op jit(solution)/shard_map/ppermute | solution.py:328
  45.6 18.9 %collective-permute-start.16 = (bf16[512,1024]{1,0:T(8,128)(2,1)S(1)}, bf16[512,1024]{1,0:T(8,128)(2,1)S(1)}, u32[]{:S(2)}, u32[]{:S(2)}) collective-permute-start(bf16[512,1024]{1,0:T(8,128)(2,1)S(1)} %collective-permute-done.8), channel_id=1, source_target_pairs={{0,1},{1,2},{2,3},{3,0},{8,11},{9,8},{10,9},{11,10},{4,5},{5,6},{6... | collective-permute-start | bytes 3145736 | tf_op jit(solution)/shard_map/ppermute | solution.py:329
  49.8 7.9 %collective-permute-start.12 = (bf16[512,256]{1,0:T(8,128)(2,1)S(1)}, bf16[512,256]{1,0:T(8,128)(2,1)S(1)}, u32[]{:S(2)}, u32[]{:S(2)}) collective-permute-start(bf16[512,256]{1,0:T(8,128)(2,1)S(1)} %collective-permute-done.10.refs_3_), channel_id=1, source_target_pairs={{0,16},{16,0},{1,17},{17,1},{2,18},{18,2},{3,19},{19,3},{4,20},{20... | collective-permute-start | bytes 786440 | tf_op jit(solution)/shard_map/ppermute | solution.py:326
  57.7 21.1 %collective-permute-start.20 = (bf16[1024,1024]{1,0:T(8,128)(2,1)S(1)}, bf16[1024,1024]{1,0:T(8,128)(2,1)S(1)}, u32[]{:S(2)}, u32[]{:S(2)}) collective-permute-start(bf16[1024,1024]{1,0:T(8,128)(2,1)S(1)} %collective-permute-done.13.w_first), channel_id=1, source_target_pairs={{0,8},{8,0},{1,9},{9,1},{2,10},{10,2},{3,11},{11,3},{4,12},{12,4},... | collective-permute-start | bytes 6291464 | tf_op jit(solution)/shard_map/ppermute | solution.py:325
  60.2 3.3 %collective-permute-start.15 = (f32[256,128]{1,0:T(8,128)S(1)}, f32[256,128]{1,0:T(8,128)S(1)}, u32[]{:S(2)}, u32[]{:S(2)}) collective-permute-start(f32[256,128]{1,0:T(8,128)S(1)} %get-tuple-element.260), channel_id=1, source_target_pairs={{0,8},{8,0},{1,9},{9,1},{2,10},{10,2},{3,11},{11,3},{4,12},{12,4},... | collective-permute-start | bytes 393224 | tf_op jit(solution)/shard_map/ppermute | solution.py:325
  60.8 2.7 %collective-permute-start.14 = (bf16[256,512]{1,0:T(8,128)(2,1)S(1)}, bf16[256,512]{1,0:T(8,128)(2,1)S(1)}, u32[]{:S(2)}, u32[]{:S(2)}) collective-permute-start(bf16[256,512]{1,0:T(8,128)(2,1)S(1)} %get-tuple-element.259), channel_id=1, source_target_pairs={{0,8},{8,0},{1,9},{9,1},{2,10},{10,2},{3,11},{11,3},{4,12},{12,4},... | collective-permute-start | bytes 786440 | tf_op jit(solution)/shard_map/ppermute | solution.py:325
  64.5 14.3 %collective-permute-start.21 = (bf16[512,1024]{1,0:T(8,128)(2,1)S(1)}, bf16[512,1024]{1,0:T(8,128)(2,1)S(1)}, u32[]{:S(2)}, u32[]{:S(2)}) collective-permute-start(bf16[512,1024]{1,0:T(8,128)(2,1)S(1)} %collective-permute-done.16.w_mine), channel_id=1, source_target_pairs={{0,8},{8,0},{1,9},{9,1},{2,10},{10,2},{3,11},{11,3},{4,12},{12,4},... | collective-permute-start | bytes 3145736 | tf_op jit(solution)/shard_map/ppermute | solution.py:325
  64.8 6.8 %collective-permute-start.17 = (bf16[128,512]{1,0:T(8,128)(2,1)S(1)}, bf16[128,512]{1,0:T(8,128)(2,1)S(1)}, u32[]{:S(2)}, u32[]{:S(2)}) collective-permute-start(bf16[128,512]{1,0:T(8,128)(2,1)S(1)} %get-tuple-element.264.own), channel_id=1, source_target_pairs={{0,1},{1,2},{2,3},{3,0},{8,11},{9,8},{10,9},{11,10},{4,5},{5,6},{6... | collective-permute-start | bytes 393224 | tf_op jit(solution)/shard_map/ppermute | solution.py:329
  66.3 6.0 %collective-permute-start.18 = (bf16[128,512]{1,0:T(8,128)(2,1)S(1)}, bf16[128,512]{1,0:T(8,128)(2,1)S(1)}, u32[]{:S(2)}, u32[]{:S(2)}) collective-permute-start(bf16[128,512]{1,0:T(8,128)(2,1)S(1)} %get-tuple-element.264.own), channel_id=1, source_target_pairs={{0,3},{1,0},{2,1},{3,2},{8,9},{9,10},{10,11},{11,8},{4,7},{5,4},{6... | collective-permute-start | bytes 393224 | tf_op jit(solution)/shard_map/ppermute | solution.py:330
  68.0 7.1 %collective-permute-start.22 = (bf16[128,512]{1,0:T(8,128)(2,1)S(1)}, bf16[128,512]{1,0:T(8,128)(2,1)S(1)}, u32[]{:S(2)}, u32[]{:S(2)}) collective-permute-start(bf16[128,512]{1,0:T(8,128)(2,1)S(1)} %get-tuple-element.268.own), channel_id=1, source_target_pairs={{0,1},{1,2},{2,3},{3,0},{8,11},{9,8},{10,9},{11,10},{4,5},{5,6},{6... | collective-permute-start | bytes 393224 | tf_op jit(solution)/shard_map/ppermute | solution.py:329
  71.6 7.2 %collective-permute-start.19 = (bf16[128,512]{1,0:T(8,128)(2,1)S(1)}, bf16[128,512]{1,0:T(8,128)(2,1)S(1)}, u32[]{:S(2)}, u32[]{:S(2)}) collective-permute-start(bf16[128,512]{1,0:T(8,128)(2,1)S(1)} %collective-permute-done.17.first), channel_id=1, source_target_pairs={{0,1},{1,2},{2,3},{3,0},{8,11},{9,8},{10,9},{11,10},{4,5},{5,6},{6... | collective-permute-start | bytes 393224 | tf_op jit(solution)/shard_map/ppermute | solution.py:329
  72.3 8.7 %collective-permute-start.23 = (bf16[128,512]{1,0:T(8,128)(2,1)S(1)}, bf16[128,512]{1,0:T(8,128)(2,1)S(1)}, u32[]{:S(2)}, u32[]{:S(2)}) collective-permute-start(bf16[128,512]{1,0:T(8,128)(2,1)S(1)} %get-tuple-element.268.own), channel_id=1, source_target_pairs={{0,3},{1,0},{2,1},{3,2},{8,9},{9,10},{10,11},{11,8},{4,7},{5,4},{6... | collective-permute-start | bytes 393224 | tf_op jit(solution)/shard_map/ppermute | solution.py:330
  75.2 6.2 %collective-permute-start.24 = (bf16[128,512]{1,0:T(8,128)(2,1)S(1)}, bf16[128,512]{1,0:T(8,128)(2,1)S(1)}, u32[]{:S(2)}, u32[]{:S(2)}) collective-permute-start(bf16[128,512]{1,0:T(8,128)(2,1)S(1)} %collective-permute-done.22.first), channel_id=1, source_target_pairs={{0,1},{1,2},{2,3},{3,0},{8,11},{9,8},{10,9},{11,10},{4,5},{5,6},{6... | collective-permute-start | bytes 393224 | tf_op jit(solution)/shard_map/ppermute | solution.py:329
  79.5 8.1 %collective-permute-start.25 = (bf16[128,1024]{1,0:T(8,128)(2,1)S(1)}, bf16[128,1024]{1,0:T(8,128)(2,1)S(1)}, u32[]{:S(2)}, u32[]{:S(2)}) collective-permute-start(bf16[128,1024]{1,0:T(8,128)(2,1)S(1)} %project.6), channel_id=1, source_target_pairs={{0,4},{4,0},{1,5},{5,1},{2,6},{6,2},{3,7},{7,3},{8,12},{12,8},{9,1... | collective-permute-start | bytes 786440 | tf_op jit(solution)/shard_map/ppermute | solution.py:327
  82.1 8.4 %collective-permute-start.26 = (bf16[128,1024]{1,0:T(8,128)(2,1)S(1)}, bf16[128,1024]{1,0:T(8,128)(2,1)S(1)}, u32[]{:S(2)}, u32[]{:S(2)}) collective-permute-start(bf16[128,1024]{1,0:T(8,128)(2,1)S(1)} %project.7), channel_id=1, source_target_pairs={{0,4},{4,0},{1,5},{5,1},{2,6},{6,2},{3,7},{7,3},{8,12},{12,8},{9,1... | collective-permute-start | bytes 786440 | tf_op jit(solution)/shard_map/ppermute | solution.py:327
